TPU v7x, 32 devices: a whole 2x2x4 slice. The times are simulated.
32 devices in a mesh: grp: 2 (over x), hor: 8 (over z, y), dep: 2 (over core).
Axes of the slice: x: 2, y: 2, z: 4, core: 2. Of those that a mesh axis runs over, the one named last changes fastest.
Arguments:
- residual: float32 [64, 64, 1024], P(('grp', 'dep'), 'hor'), parts along dimension 0, may hold values from -6 to 6
- focus_bins: int32 [64, 64, 1024], P(('grp', 'dep'), 'hor'), parts along dimension 0, may hold values from 0 to 15
- layer_class: int32 [64], P('grp'), parts along dimension 0, may hold values from 0 to 7
Outputs:
- preconditioned: float32 [64, 64, 1024], P(('grp', 'dep'), 'hor'), parts along dimension 0
There are 2 independent parts, one for each index of `grp`. A program takes and returns all parts, laid end to end along the dimension named above; each array names one. Nothing has to cross between parts.
All inputs are finite; a program needn't handle non-finite values.
Results may differ from a plain program's by a relative error of at most 0.0003.
Values sent between devices are 32-bit elements; how exact they have to be, the bound alone decides.
A program may use at most 128 MiB of HBM per device.

v0:
```python
import math

import jax
import jax.numpy as jnp
from jax import lax
from jax.sharding import PartitionSpec as P

damping = 0.01
smoothing = 1.0
coupling_scale = 1.0
weight_base = 0.5
weight_step = 0.2
focus_base = 0.5
focus_step = 0.09242
highest = lax.Precision.HIGHEST


def partner_2(value, axis, distance):
    mask = 2**distance
    pairs = [(source, source ^ mask) for source in range(lax.axis_size(axis))]
    return lax.ppermute(value, axis, pairs)


def depth_weights(layer_class):
    return weight_base * jnp.exp(weight_step * layer_class.astype(jnp.float32))


def focusing(focus_bins):
    return focus_base * jnp.exp(focus_step * focus_bins.astype(jnp.float32))


def couplings(weights):
    inner = coupling_scale * weights[:-1] * weights[1:]
    zero_end = jnp.zeros((1,), jnp.float32)
    return (jnp.concatenate([zero_end, inner]), jnp.concatenate([inner, zero_end]))


def symbol(frequency, length):
    return 2.0 - 2.0 * jnp.cos(frequency * (2.0 * math.pi / length))


def cas_table(length):
    position = jnp.arange(length, dtype=jnp.int32)
    product = position[:, None] * position[None, :] % length
    angles = product.astype(jnp.float32) * (2.0 * math.pi / length)
    return jnp.cos(angles) + jnp.sin(angles)


def shift_down(values, distance, fill_value):
    filler = jnp.full(values.shape[:-2] + (distance, values.shape[-1]), fill_value, values.dtype)
    return jnp.concatenate([filler, values[..., :-distance, :]], axis=-2)


def shift_up(values, distance, fill_value):
    filler = jnp.full(values.shape[:-2] + (distance, values.shape[-1]), fill_value, values.dtype)
    return jnp.concatenate([values[..., distance:, :], filler], axis=-2)


def reduce_step(lower, middle, upper, source, rows_below, rows_above):
    lower_below, middle_below, upper_below, source_below = rows_below
    lower_above, middle_above, upper_above, source_above = rows_above
    ratio_below = -lower / middle_below
    ratio_above = -upper / middle_above
    new_lower = ratio_below * lower_below
    new_middle = middle + ratio_below * upper_below + ratio_above * lower_above
    new_upper = ratio_above * upper_above
    new_source = source + ratio_below * source_below + ratio_above * source_above
    return (new_lower, new_middle, new_upper, new_source)


def local_solve(lower, middle, upper, source):
    layer_count = middle.shape[0]
    distance = 1
    while distance < layer_count:
        rows_below = (
            shift_down(lower, distance, 0.0),
            shift_down(middle, distance, 1.0),
            shift_down(upper, distance, 0.0),
            shift_down(source, distance, 0.0),
        )
        rows_above = (
            shift_up(lower, distance, 0.0),
            shift_up(middle, distance, 1.0),
            shift_up(upper, distance, 0.0),
            shift_up(source, distance, 0.0),
        )
        lower, middle, upper, source = reduce_step(
            lower, middle, upper, source, rows_below, rows_above
        )
        distance = distance * 2
    return source / middle


def body(residual, focus_bins, layer_class):
    depth_rows, y_rows, x_cells = residual.shape
    hor_count = lax.axis_size("hor")
    y_cells = y_rows * hor_count
    focus_map = focusing(focus_bins)
    scaled = focus_map * residual
    weights = depth_weights(layer_class)
    couple_prev, couple_next = couplings(weights)
    first_row = lax.axis_index("dep") * depth_rows
    table_x = cas_table(x_cells)
    table_y = cas_table(y_cells)
    symbol_y = symbol(jnp.arange(y_cells, dtype=jnp.float32), y_cells)
    block_width = x_cells // hor_count
    block_index = lax.axis_index("hor")
    spectra = jnp.einsum(
        "zcx,xbj->bzcj", scaled, table_x.reshape(x_cells, hor_count, block_width), precision=highest
    )
    spectra = spectra.reshape(hor_count, depth_rows, y_rows * block_width)
    table_rows = table_y.reshape(hor_count, y_rows, y_cells)
    portion = lax.all_to_all(spectra, "hor", split_axis=0, concat_axis=0, tiled=True)
    item_count = portion.shape[1]
    arranged = portion.reshape(hor_count, item_count, y_rows, block_width)
    spectrum = jnp.einsum("hzcj,hcy->zjy", arranged, table_rows, precision=highest)
    spectrum = spectrum.reshape(depth_rows, block_width * y_cells)
    wave_x = (block_index * block_width + jnp.arange(block_width, dtype=jnp.int32)).astype(
        jnp.float32
    )
    wave_term = (
        damping + smoothing * (symbol_y[None, :] + symbol(wave_x, x_cells)[:, None])
    ).reshape(-1)
    weight_local = lax.dynamic_slice_in_dim(weights, first_row, depth_rows)
    prev_local = lax.dynamic_slice_in_dim(couple_prev, first_row, depth_rows)
    next_local = lax.dynamic_slice_in_dim(couple_next, first_row, depth_rows)
    middle = weight_local[:, None] * wave_term[None, :] + (prev_local + next_local)[:, None]
    lower = jnp.broadcast_to(-prev_local[:, None], middle.shape)
    upper = jnp.broadcast_to(-next_local[:, None], middle.shape)
    row_index = jnp.arange(depth_rows, dtype=jnp.int32)
    edge_term = jnp.where(row_index == 0, prev_local[0], 0.0) + jnp.where(
        row_index == depth_rows - 1, next_local[depth_rows - 1], 0.0
    )
    source = jnp.stack([spectrum, jnp.broadcast_to(edge_term[:, None], spectrum.shape)])
    solutions = local_solve(lower, middle, upper, source)
    base_part = solutions[0]
    response = solutions[1]
    edge_row = (1 - lax.axis_index("dep")) * (depth_rows - 1)
    base_edge = lax.dynamic_index_in_dim(base_part, edge_row, 0, keepdims=False)
    response_edge = lax.dynamic_index_in_dim(response, edge_row, 0, keepdims=False)
    partner = partner_2(jnp.stack([base_edge, response_edge]), "dep", 0)
    divisor = 1.0 - response_edge * partner[1]
    interface = (partner[0] + partner[1] * base_edge) / divisor
    solved = base_part + response * interface[None, :]
    solved = solved.reshape(depth_rows, block_width, y_cells)
    returned = jnp.einsum(
        "zjk,khc->hzcj", solved, table_y.reshape(y_cells, hor_count, y_rows), precision=highest
    )
    returned = returned.reshape(hor_count, depth_rows, y_rows * block_width)
    table_back = table_x.reshape(hor_count, block_width, x_cells)
    portion = lax.all_to_all(returned, "hor", split_axis=0, concat_axis=0, tiled=True)
    item_count = portion.shape[1]
    arranged = portion.reshape(hor_count, item_count, y_rows, block_width)
    result_field = jnp.einsum("bzcj,bjx->zcx", arranged, table_back, precision=highest)
    return focus_map * result_field / (x_cells * y_cells)


def solution(mesh):
    return jax.shard_map(
        body,
        mesh=mesh,
        in_specs=(P(("grp", "dep"), "hor", None), P(("grp", "dep"), "hor", None), P("grp")),
        out_specs=P(("grp", "dep"), "hor", None),
        check_vma=False,
    )
```

profile of v0, /device:TPU:0, one launch (start us, length us, event | category | flops | bytes accessed | tf_op | source)
XLA Modules:
  0.0 95.7 jit_solution(13671068101681887568)
XLA Ops:
  0.0 1.3 %fusion.57 = f32[16,8,1024]{2,1,0:T(8,128)S(1)} fusion(f32[16,8,1024]{2,1,0:T(8,128)} %param.3, s32[16,8,1024]{2,1,0:T(8,128)} %param.4), kind=kLoop, calls=%fused_computation.81 | loop fusion | flops 524288 | bytes 1572864 | tf_op jit(solution)/shard_map/mul | solution.py:99
  1.3 20.2 %fusion.36 = f32[8,8,2,8,128]{4,3,2,1,0:T(8,128)S(1)} fusion(s32[8,128]{1,0:T(8,128)S(1)} %multiply_add_fusion.8, f32[16,8,1024]{2,1,0:T(8,128)S(1)} %fusion.57), kind=kOutput, calls=%fused_computation.44 | convolution fusion | flops 1626341376 | bytes 1052672 | tf_op jit(solution)/shard_map/zcx,xbj->bzcj/dot_general | solution.py:108
  21.5 0.9 copy.34
  22.4 7.3 %all-to-all-start = ((f32[8,16,1024]{2,1,0:T(8,128)}), f32[8,16,1024]{2,1,0:T(8,128)}, u32[]{:S(2)}, u32[]{:S(2)}) async-start(f32[8,16,1024]{2,1,0:T(8,128)} %bitcast.76), calls=%async_computation | async-start | bytes 1048576 | tf_op jit(solution)/shard_map/all_to_all | solution.py:113
  29.9 0.1 pad_maximum_fusion.2
  29.9 0.1 fusion.97
  30.1 0.1 add_add_fusion
  30.2 0.1 add.306
  30.3 0.1 multiply_add_fusion.7
  30.7 0.1 broadcast_multiply_fusion
  31.0 0.1 broadcast_multiply_fusion.1
  31.1 0.2 multiply_add_fusion.6
  31.4 0.5 copy-done
  32.0 0.1 pad_multiply_fusion.2
  32.2 0.2 pad_multiply_fusion.3
  32.3 0.2 multiply_add_fusion.5
  32.7 0.2 pad_multiply_fusion.1
  32.9 0.1 pad_multiply_fusion
  33.0 0.2 multiply_add_fusion.4
  33.3 1.2 %multiply_add_fusion.3 = (f32[16,8192]{1,0:T(8,128)}, f32[16,8192]{1,0:T(8,128)}, f32[16,8192]{1,0:T(8,128)}) fusion(f32[8,8192]{1,0:T(8,128)S(1)} %slice.184, f32[16,8192]{1,0:T(8,128)S(1)} %multiply_add_fusion.4, f32[8,8192]{1,0:T(8,128)S(1)} %slice.183, f32[8,8192]{1,0:T(8,128)S(1)} %get-tuple-element.35, f32[16,8192]{1,0:T(8,128)S(1)} %get-tuple-element.8, ...), kind=kLoop, calls=%fused_computation.63 | loop fusion | flops 1048576 | bytes 4194304 | tf_op jit(solution)/shard_map/add | solution.py:65
  34.5 0.6 slice.122
  35.2 0.6 fusion.84
  35.8 0.2 add_bitcast_fusion
  36.0 8.2 %all-to-all-done = f32[8,16,1024]{2,1,0:T(8,128)} async-done(((f32[8,16,1024]{2,1,0:T(8,128)}), f32[8,16,1024]{2,1,0:T(8,128)}, u32[]{:S(2)}, u32[]{:S(2)}) %all-to-all-start) | async-done | bytes 524320 | tf_op jit(solution)/shard_map/all_to_all | solution.py:113
  44.2 1.1 %copy.25 = f32[16,8,8,128]{3,2,1,0:T(8,128)S(1)} copy(f32[16,8,8,128]{3,1,2,0:T(8,128)} %bitcast.29) | data formatting | bytes 1048576
  45.4 2.8 %convolution_bitcast_fusion = f32[16,128,64]{2,1,0:T(8,128)} fusion(f32[8,8,64,1]{2,0,1,3:T(8,128)S(1)} %add_bitcast_fusion, f32[8,16,8,128]{3,2,1,0:T(8,128)S(1)} %bitcast.83), kind=kOutput, calls=%fused_computation.43 | convolution fusion | flops 100663296 | bytes 1064960 | tf_op jit(solution)/shard_map/hzcj,hcy->zjy/dot_general | solution.py:116
  48.2 1.6 %stack_reshape.3 = f32[1,16,8192]{2,1,0:T(8,128)S(1)} reshape(f32[16,128,64]{2,1,0:T(8,128)} %convolution_bitcast_fusion) | data formatting | bytes 1048576 | tf_op jit(solution)/shard_map/stack;reshape | solution.py:134
  49.7 0.1 stack_broadcast_in_dim.2
  49.9 0.1 fusion.48
  50.0 0.9 copy-done.1
  50.9 0.3 fusion.51
  51.2 0.1 fusion.102
  51.3 0.3 multiply_add_fusion.1
  51.6 0.1 fusion.101
  51.7 0.3 multiply_add_fusion
  52.1 0.9 copy-done.2
  53.0 0.2 copy-done.3
  53.2 0.2 copy-done.4
  53.4 0.2 add_divide_fusion
  53.9 1.2 %collective-permute-done = f32[2,8192]{1,0:T(2,128)S(1)} collective-permute-done((f32[2,8192]{1,0:T(2,128)S(1)}, f32[2,8192]{1,0:T(2,128)S(1)}, u32[]{:S(2)}, u32[]{:S(2)}) %collective-permute-start) | collective-permute-done | bytes 65568 | tf_op jit(solution)/shard_map/ppermute | solution.py:21
  55.1 0.1 fusion.64
  55.2 0.1 multiply_add_fusion.2
  55.3 0.4 add.329
  55.7 1.4 %convolution_bitcast_fusion.1 = f32[8,16,8,128]{3,2,1,0:T(8,128)S(1)} fusion(f32[16,128,64]{2,1,0:T(8,128)S(1)} %add.329, s32[8,8]{1,0:T(8,128)S(1)} %multiply_add_fusion.9), kind=kOutput, calls=%fused_computation.46 | convolution fusion | flops 100724736 | bytes 1048832 | tf_op jit(solution)/shard_map/zjk,khc->hzcj/dot_general | solution.py:146
  57.2 0.1 reshape.255
  57.3 18.4 %all_to_all.10 = f32[8,16,1024]{2,1,0:T(8,128)S(1)} all-to-all(f32[8,16,1024]{2,1,0:T(8,128)S(1)} %reshape.255), channel_id=1, replica_groups=mesh['grp'=2,'hor'=8,'dep'=2] {'hor'}, dimensions={0} | all-to-all | bytes 1048576 | tf_op jit(solution)/shard_map/all_to_all | solution.py:151
  75.6 0.1 copy.26
  75.7 19.9 %fusion.45 = f32[16,8,1024]{2,1,0:T(8,128)} fusion(s32[8,128]{1,0:T(8,128)S(1)} %multiply_add_fusion.8, s32[16,8,1024]{2,1,0:T(8,128)S(1)} %copy-done.5, f32[8,16,8,128]{3,2,1,0:T(8,128)S(1)} %bitcast.84), kind=kOutput, calls=%fused_computation.48 | convolution fusion | flops 1626996736 | bytes 1576960 | tf_op jit(solution)/shard_map/bzcj,bjx->zcx/dot_general | solution.py:154
  (40 shorter events, 1.6 us)
Async XLA Ops:
  21.5 8.2 %copy-start.6 = (s32[32]{0:T(128)S(1)}, s32[32]{0:T(128)}, u32[]{:S(2)}) copy-start(s32[32]{0:T(128)} %param.5) | copy-start | bytes 388
  22.4 21.9 %all-to-all-start = ((f32[8,16,1024]{2,1,0:T(8,128)}), f32[8,16,1024]{2,1,0:T(8,128)}, u32[]{:S(2)}, u32[]{:S(2)}) async-start(f32[8,16,1024]{2,1,0:T(8,128)} %bitcast.76), calls=%async_computation | async-start | bytes 1048576 | tf_op jit(solution)/shard_map/all_to_all | solution.py:113
  31.1 0.8 copy-start
  49.8 1.0 %copy-start.1 = (f32[16,8192]{1,0:T(8,128)S(1)}, f32[16,8192]{1,0:T(8,128)}, u32[]{:S(2)}) copy-start(f32[16,8192]{1,0:T(8,128)} %copy-done) | copy-start | bytes 1572868
  52.0 1.0 %copy-start.2 = (f32[16,8192]{1,0:T(8,128)S(1)}, f32[16,8192]{1,0:T(8,128)}, u32[]{:S(2)}) copy-start(f32[16,8192]{1,0:T(8,128)} %get-tuple-element.5) | copy-start | bytes 1572868
  52.0 1.2 %copy-start.3 = (f32[16,8192]{1,0:T(8,128)S(1)}, f32[16,8192]{1,0:T(8,128)}, u32[]{:S(2)}) copy-start(f32[16,8192]{1,0:T(8,128)} %get-tuple-element.6) | copy-start | bytes 1572868
  52.0 1.3 %copy-start.4 = (f32[16,8192]{1,0:T(8,128)S(1)}, f32[16,8192]{1,0:T(8,128)}, u32[]{:S(2)}) copy-start(f32[16,8192]{1,0:T(8,128)} %get-tuple-element.7) | copy-start | bytes 1572868
  53.8 1.3 %collective-permute-start = (f32[2,8192]{1,0:T(2,128)S(1)}, f32[2,8192]{1,0:T(2,128)S(1)}, u32[]{:S(2)}, u32[]{:S(2)}) collective-permute-start(f32[2,8192]{1,0:T(2,128)S(1)} %pad_maximum_fusion.1), channel_id=1, source_target_pairs={{0,1},{1,0},{2,3},{3,2},{4,5},{5,4},{6,7},{7,6},{8,9},{9,8},{10,11... | collective-permute-start | bytes 196616 | tf_op jit(solution)/shard_map/ppermute | solution.py:21
  57.2 18.5 %copy-start.5 = (s32[16,8,1024]{2,1,0:T(8,128)S(1)}, s32[16,8,1024]{2,1,0:T(8,128)}, u32[]{:S(2)}) copy-start(s32[16,8,1024]{2,1,0:T(8,128)} %param.4) | copy-start | bytes 1572868
where the time goes:
time: 96.1 us; the launch traced here: 95.7 us
  matrix products  44.3 us (46%)
  blocking collectives  18.4 us (19%)
  waiting for transfers between devices  9.43 us (10%)
  local copies, waits for them, and re-layouts  9.11 us (9%)
  starting transfers between devices  7.35 us (8%)
  other arithmetic  6.73 us (7%)
    dot_general x1, matrix products, body(): jnp.einsum('zcx,xbj->bzcj', scaled, table_x.reshape(x_cells, hor_count, b...  20.2 us
    dot_general x1, matrix products, body(): jnp.einsum('bzcj,bjx->zcx', arranged, table_back, precision=highest)  19.9 us
    all_to_all x1, blocking collectives, body(): lax.all_to_all(returned, 'hor', split_axis=0, concat_axis=0, tiled=True)  18.4 us
    all_to_all x1, waiting for transfers between devices, body(): lax.all_to_all(spectra, 'hor', split_axis=0, concat_axis=0, tiled=True)  8.19 us
    all_to_all x1, starting transfers between devices, body(): lax.all_to_all(spectra, 'hor', split_axis=0, concat_axis=0, tiled=True)  7.28 us
    unnamed x16, local copies, waits for them, and re-layouts  3.92 us
    dot_general x1, matrix products, body(): jnp.einsum('hzcj,hcy->zjy', arranged, table_rows, precision=highest)  2.79 us
  transfers between devices with their start and end apart: 2, of which 2 were waited for; matrix products, arithmetic and copies ran while one was open for 6% of the time, Pallas kernels for 0%

commit v1 on v0

--- a/solution.py
+++ b/solution.py
@@ -1,8 +1,13 @@
+import functools
 import math
 
 import jax
 import jax.numpy as jnp
+import ml_dtypes
+import numpy as np
 from jax import lax
+from jax.experimental import pallas as pl
+from jax.experimental.pallas import tpu as pltpu
 from jax.sharding import PartitionSpec as P
 
 damping = 0.01
@@ -154,10 +159,378 @@
     result_field = jnp.einsum("bzcj,bjx->zcx", arranged, table_back, precision=highest)
     return focus_map * result_field / (x_cells * y_cells)
 
+MESH = pl.DeviceIdType.MESH
+GROUP = 4
+
+
+def split_table(length):
+    position = np.arange(length)
+    angles = (position[:, None] * position[None, :] % length) * (2.0 * math.pi / length)
+    table = np.cos(angles) + np.sin(angles)
+    high = table.astype(ml_dtypes.bfloat16)
+    low = (table - high.astype(np.float64)).astype(ml_dtypes.bfloat16)
+    return high, low
+
+
+def split_values(values):
+    high = values.astype(jnp.bfloat16)
+    low = (values - high.astype(jnp.float32)).astype(jnp.bfloat16)
+    return high, low
+
+
+def dot32(left, right):
+    return jnp.dot(left, right, preferred_element_type=jnp.float32)
+
+
+def pair_order(mine):
+    beside = mine + 1 - 2 * lax.rem(mine, 2)
+    return [lax.rem(mine + 2, 4), 3 - mine, beside, mine]
+
+
+def kernel(
+    residual,
+    bins,
+    classes,
+    table_high,
+    table_low,
+    table_y,
+    wave_x,
+    wave_y,
+    field,
+    res_v,
+    bins_v,
+    high_v,
+    low_v,
+    send_a,
+    recv_a,
+    send_b,
+    recv_b,
+    weights,
+    spectrum,
+    inverse,
+    factor,
+    edge_out,
+    edge_in,
+    load_sem,
+    high_sem,
+    low_sem,
+    send_a_sem,
+    recv_a_sem,
+    send_b_sem,
+    recv_b_sem,
+    edge_send_sem,
+    edge_recv_sem,
+):
+    count, layers, y_rows, width = send_a.shape
+    y_cells = count * y_rows
+    rows = layers * y_rows
+    me = lax.axis_index("hor")
+    half = lax.axis_index("dep")
+    order = pair_order(me // 2)
+
+    loads = [
+        pltpu.make_async_copy(residual, res_v, load_sem.at[0]),
+        pltpu.make_async_copy(bins, bins_v, load_sem.at[1]),
+    ]
+    for load in loads:
+        load.start()
+    table_loads = []
+    for pair in order:
+        both = [
+            pltpu.make_async_copy(table_high.at[pair], high_v.at[pair], high_sem.at[pair]),
+            pltpu.make_async_copy(table_low.at[pair], low_v.at[pair], low_sem.at[pair]),
+        ]
+        for load in both:
+            load.start()
+        table_loads.append(both)
+
+    barrier = pltpu.get_barrier_semaphore()
+    for step in range(1, count):
+        pl.semaphore_signal(
+            barrier, inc=1, device_id={"hor": lax.rem(me + step, count)}, device_id_type=MESH
+        )
+    pl.semaphore_signal(barrier, inc=1, device_id={"dep": 1 - half}, device_id_type=MESH)
+
+    for load in loads:
+        load.wait()
+    focus_map = focus_base * jnp.exp(focus_step * bins_v[...].astype(jnp.float32))
+    scaled = (focus_map * res_v[...]).reshape(rows, count * width)
+    high, low = split_values(scaled)
+    stacked = jnp.concatenate([high, low], axis=0)
+
+    def send_forward(target):
+        return pltpu.make_async_remote_copy(
+            src_ref=send_a.at[target],
+            dst_ref=recv_a.at[me],
+            send_sem=send_a_sem.at[target],
+            recv_sem=recv_a_sem.at[me],
+            device_id={"hor": target},
+            device_id_type=MESH,
+        )
+
+    other = me + 1 - 2 * lax.rem(me, 2)
+    for step, pair in enumerate(order):
+        for load in table_loads[step]:
+            load.wait()
+        first = dot32(stacked, high_v[pair])
+        value = first[:rows] + first[rows:] + dot32(high, low_v[pair])
+        send_a[2 * pair] = value[:, :width].reshape(layers, y_rows, width)
+        send_a[2 * pair + 1] = value[:, width:].reshape(layers, y_rows, width)
+        if step == 0:
+            pl.semaphore_wait(barrier, count)
+        if step < 3:
+            send_forward(2 * pair).start()
+            send_forward(2 * pair + 1).start()
+        else:
+            send_forward(other).start()
+    recv_a[me] = send_a[me]
+
+    for layer in range(2 * layers):
+        index = jnp.full((8, width), classes[0, layer], jnp.int32).astype(jnp.float32)
+        weights[layer] = weight_base * jnp.exp(weight_step * index)
+
+    def layer_of(place):
+        return place + half * (layers - 1 - 2 * place)
+
+    def coupling_after(place):
+        here = half * layers + layer_of(place)
+        return coupling_scale * weights[here] * weights[here + 1 - 2 * half]
+
+    wave = (damping + smoothing * (wave_y[...] + wave_x[me][None])).reshape(y_cells // 8, 8, width)
+
+    def pivot_step(place, carried):
+        excess_part = carried
+        here = weights[half * layers + layer_of(place)]
+        excess = here[None] * wave + excess_part
+        after = coupling_after(place)[None]
+        reciprocal = 1.0 / (excess + after)
+        inverse[place] = reciprocal
+        scaled_after = after * reciprocal
+        factor[place] = scaled_after
+        edge_out[0] = excess
+        return scaled_after * excess
+
+    lax.fori_loop(0, layers, pivot_step, jnp.zeros_like(wave))
+
+    def edge_copy(slot):
+        return pltpu.make_async_remote_copy(
+            src_ref=edge_out.at[slot],
+            dst_ref=edge_in.at[slot],
+            send_sem=edge_send_sem.at[slot],
+            recv_sem=edge_recv_sem.at[slot],
+            device_id={"dep": 1 - half},
+            device_id_type=MESH,
+        )
+
+    edge_copy(0).start()
+
+    for step in range(1, count):
+        source = lax.rem(me + step, count)
+        pltpu.make_async_remote_copy(
+            src_ref=send_a.at[source],
+            dst_ref=recv_a.at[source],
+            send_sem=send_a_sem.at[source],
+            recv_sem=recv_a_sem.at[source],
+            device_id={"hor": source},
+            device_id_type=MESH,
+        ).wait_recv()
+
+    def transform_y(first, second):
+        values = jnp.concatenate([first, second], axis=1)
+        upper, lower = split_values(values)
+        return dot32(table_y[...], jnp.concatenate([upper, upper, lower], axis=0))
+
+    def spectrum_step(index, carried):
+        first = recv_a[:, 2 * index].reshape(y_cells, width)
+        second = recv_a[:, 2 * index + 1].reshape(y_cells, width)
+        value = transform_y(first, second)
+        spectrum[2 * index] = value[:, :width].reshape(y_cells // 8, 8, width)
+        spectrum[2 * index + 1] = value[:, width:].reshape(y_cells // 8, 8, width)
+        return carried
+
+    lax.fori_loop(0, layers // 2, spectrum_step, 0)
+
+    def forward_step(place, carried):
+        here = spectrum[layer_of(place)] + carried
+        spectrum[layer_of(place)] = here
+        return factor[place] * here
+
+    lax.fori_loop(0, layers - 1, forward_step, jnp.zeros_like(wave))
+    edge_out[1] = spectrum[layer_of(layers - 1)] + factor[layers - 2] * spectrum[layer_of(layers - 2)]
+    edge_copy(1).start()
+    edge_copy(0).wait()
+    excess_here = edge_out[0]
+    excess_there = edge_in[0]
+    after = coupling_after(layers - 1)[None]
+    scale = 1.0 / (excess_here * excess_there + after * (excess_here + excess_there))
+    edge_copy(1).wait()
+    last = ((excess_there + after) * edge_out[1] + after * edge_in[1]) * scale
+    spectrum[layer_of(layers - 1)] = last
+
+    def send_back(group, target):
+        start = group * GROUP + half * (layers - GROUP - 2 * group * GROUP)
+        return pltpu.make_async_remote_copy(
+            src_ref=send_b.at[target, pl.ds(start, GROUP)],
+            dst_ref=recv_b.at[me, pl.ds(start, GROUP)],
+            send_sem=send_b_sem.at[group, target],
+            recv_sem=recv_b_sem.at[group, me],
+            device_id={"hor": target},
+            device_id_type=MESH,
+        )
+
+    def wait_back(group, source):
+        start = group * GROUP + half * (layers - GROUP - 2 * group * GROUP)
+        pltpu.make_async_remote_copy(
+            src_ref=send_b.at[source, pl.ds(start, GROUP)],
+            dst_ref=recv_b.at[source, pl.ds(start, GROUP)],
+            send_sem=send_b_sem.at[group, source],
+            recv_sem=recv_b_sem.at[group, source],
+            device_id={"hor": source},
+            device_id_type=MESH,
+        ).wait_recv()
+
+    def backward_step(place, following):
+        here = layer_of(place)
+        value = inverse[place] * spectrum[here] + factor[place] * following
+        spectrum[here] = value
+        return value
+
+    following = last
+    groups = layers // GROUP
+    for group in reversed(range(groups)):
+        for place in reversed(range(group * GROUP, (group + 1) * GROUP)):
+            if place < layers - 1:
+                following = backward_step(place, following)
+        for place in range(group * GROUP, (group + 1) * GROUP, 2):
+            first = layer_of(place)
+            second = layer_of(place + 1)
+            value = transform_y(
+                spectrum[first].reshape(y_cells, width), spectrum[second].reshape(y_cells, width)
+            )
+            send_b[:, first] = value[:, :width].reshape(count, y_rows, width)
+            send_b[:, second] = value[:, width:].reshape(count, y_rows, width)
+        for pair in order[:3]:
+            send_back(group, 2 * pair).start()
+            send_back(group, 2 * pair + 1).start()
+        send_back(group, other).start()
+    recv_b[me] = send_b[me]
+
+    for step, pair in enumerate(reversed(order)):
+        for group in reversed(range(groups)):
+            if step > 0:
+                wait_back(group, 2 * pair)
+                wait_back(group, 2 * pair + 1)
+            else:
+                wait_back(group, other)
+        value = jnp.concatenate(
+            [recv_b[2 * pair].reshape(rows, width), recv_b[2 * pair + 1].reshape(rows, width)],
+            axis=1,
+        )
+        upper, lower = split_values(value)
+        stacked = jnp.concatenate([upper, lower], axis=0)
+        start = pl.multiple_of(pair * 2 * width, 2 * width)
+        for block in range(count // 2):
+            first = dot32(stacked, high_v[block, pl.ds(start, 2 * width)])
+            total = first[:rows] + first[rows:] + dot32(upper, low_v[block, pl.ds(start, 2 * width)])
+            columns = slice(block * 2 * width, (block + 1) * 2 * width)
+            total = total.reshape(layers, y_rows, 2 * width)
+            if step > 0:
+                total = total + field[:, :, columns]
+            field[:, :, columns] = total
+
+    for step in range(1, count):
+        target = lax.rem(me + step, count)
+        send_forward(target).wait_send()
+        for group in range(groups):
+            send_back(group, target).wait_send()
+
+
+def kernel_body(residual, focus_bins, layer_class):
+    layers, y_rows, x_cells = residual.shape
+    count = lax.axis_size("hor")
+    width = x_cells // count
+    y_cells = y_rows * count
+    high, low = split_table(x_cells)
+    high = np.ascontiguousarray(high.reshape(x_cells, count // 2, 2 * width).transpose(1, 0, 2))
+    low = np.ascontiguousarray(low.reshape(x_cells, count // 2, 2 * width).transpose(1, 0, 2))
+    high_y, low_y = split_table(y_cells)
+    table_y = np.concatenate([high_y, low_y, high_y], axis=1)
+    wave_x = 2.0 - 2.0 * np.cos(np.arange(x_cells) * (2.0 * math.pi / x_cells))
+    wave_x = np.broadcast_to(wave_x.reshape(count, 1, width), (count, 8, width))
+    wave_x = np.tile(wave_x, (1, y_cells // 8, 1)).astype(np.float32)
+    wave_y = 2.0 - 2.0 * np.cos(np.arange(y_cells) * (2.0 * math.pi / y_cells))
+    wave_y = np.broadcast_to(wave_y[:, None], (y_cells, width)).astype(np.float32)
+    block = (count, layers, y_rows, width)
+    column = (layers, y_cells // 8, 8, width)
+    f32, dma = jnp.float32, pltpu.SemaphoreType.DMA
+    hbm = pl.BlockSpec(memory_space=pl.ANY)
+    vmem = pl.BlockSpec(memory_space=pltpu.VMEM)
+    smem = pl.BlockSpec(memory_space=pltpu.SMEM)
+    field = pl.pallas_call(
+        kernel,
+        out_shape=jax.ShapeDtypeStruct(residual.shape, f32),
+        in_specs=[hbm, hbm, smem, hbm, hbm, vmem, vmem, vmem],
+        out_specs=vmem,
+        scratch_shapes=[
+            pltpu.VMEM(residual.shape, f32),
+            pltpu.VMEM(residual.shape, jnp.int32),
+            pltpu.VMEM(high.shape, jnp.bfloat16),
+            pltpu.VMEM(low.shape, jnp.bfloat16),
+            pltpu.VMEM(block, f32),
+            pltpu.VMEM(block, f32),
+            pltpu.VMEM(block, f32),
+            pltpu.VMEM(block, f32),
+            pltpu.VMEM((2 * layers, 8, width), f32),
+            pltpu.VMEM(column, f32),
+            pltpu.VMEM(column, f32),
+            pltpu.VMEM(column, f32),
+            pltpu.VMEM((2,) + column[1:], f32),
+            pltpu.VMEM((2,) + column[1:], f32),
+            dma((2,)),
+            dma((count // 2,)),
+            dma((count // 2,)),
+            dma((count,)),
+            dma((count,)),
+            dma((layers // GROUP, count)),
+            dma((layers // GROUP, count)),
+            dma((2,)),
+            dma((2,)),
+        ],
+        compiler_params=pltpu.CompilerParams(
+            collective_id=0, has_side_effects=True, vmem_limit_bytes=40 * 2**20
+        ),
+        cost_estimate=pl.CostEstimate(
+            flops=2 * 6 * layers * y_rows * x_cells * x_cells,
+            bytes_accessed=6 * 2**20,
+            transcendentals=layers * y_rows * x_cells,
+        ),
+    )(
+        residual,
+        focus_bins,
+        layer_class.reshape(1, -1),
+        jnp.asarray(high),
+        jnp.asarray(low),
+        jnp.asarray(table_y),
+        jnp.asarray(wave_x),
+        jnp.asarray(wave_y),
+    )
+    return focusing(focus_bins) * field * (1.0 / (x_cells * y_cells))
+
+
+def fits_kernel(mesh):
+    return mesh.shape["hor"] == 8 and mesh.shape["dep"] == 2
+
+
+def chosen(mesh, residual, focus_bins, layer_class):
+    shape = residual.shape
+    if fits_kernel(mesh) and shape[1] % 8 == 0 and shape[2] == 1024 and shape[0] % GROUP == 0:
+        return kernel_body(residual, focus_bins, layer_class)
+    return body(residual, focus_bins, layer_class)
+
 
 def solution(mesh):
     return jax.shard_map(
-        body,
+        functools.partial(chosen, mesh),
         mesh=mesh,
         in_specs=(P(("grp", "dep"), "hor", None), P(("grp", "dep"), "hor", None), P("grp")),
         out_specs=P(("grp", "dep"), "hor", None),

time: 96.1 us -> 45.5 us (0.47)
  matrix products: 44.3 us -> 0 us
  Pallas kernels: 0 us -> 35.7 us
  blocking collectives: 18.4 us -> 0 us
  waiting for transfers between devices: 9.43 us -> 0 us
  starting transfers between devices: 7.35 us -> 0 us
  other arithmetic: 6.73 us -> 0.95 us
    dot_general x4 -> x0, matrix products: 44.3 us -> none  [the longest x1 20.2 us: body(): jnp.einsum('zcx,xbj->bzcj', scaled, table_x.reshape(x_cells, hor_count, b...]
    pallas_call x0 -> x1, Pallas kernels: none -> 35.7 us  [kernel_body(): pl.pallas_call(kernel, out_shape=jax.ShapeDtypeStruct(residual.shape, f32...]
    all_to_all x1 -> x0, blocking collectives: 18.4 us -> none  [body(): lax.all_to_all(returned, 'hor', split_axis=0, concat_axis=0, tiled=True)]
    all_to_all x1 -> x0, waiting for transfers between devices: 8.19 us -> none  [body(): lax.all_to_all(spectra, 'hor', split_axis=0, concat_axis=0, tiled=True)]
    all_to_all x1 -> x0, starting transfers between devices: 7.28 us -> none  [body(): lax.all_to_all(spectra, 'hor', split_axis=0, concat_axis=0, tiled=True)]
    unnamed x16, local copies, waits for them, and re-layouts: 3.92 us -> 8.38 us
    add x13 -> x0, other arithmetic: 3.72 us -> none  [the longest x4 1.78 us: reduce_step(): new_middle = middle + ratio_below * upper_below + ratio_above * lower_above]
    slice x17 -> x0, local copies, waits for them, and re-layouts: 1.73 us -> none  [the longest x10 0.79 us: shift_down(): return jnp.concatenate([filler, values[..., :-distance, :]], axis=-2)]
  transfers between devices with their start and end apart: 2 -> 0, of which waited for: 2 -> 0; matrix products, arithmetic and copies ran while one was open for 6% -> 0% of each run, Pallas kernels for 0% -> 0%
where the time goes in v1:
time: 45.5 us; the launch traced here: 45 us
  Pallas kernels  35.7 us (78%)
  local copies, waits for them, and re-layouts  8.38 us (18%)
  other arithmetic  0.95 us (2%)
    pallas_call x1, Pallas kernels, kernel_body(): pl.pallas_call(kernel, out_shape=jax.ShapeDtypeStruct(residual.shape, f32...  35.7 us
    unnamed x16, local copies, waits for them, and re-layouts  8.38 us
    mul x1, other arithmetic, kernel_body(): return focusing(focus_bins) * field * (1.0 / (x_cells * y_cells))  0.95 us

profile of v1, /device:TPU:0, one launch (start us, length us, event | category | flops | bytes accessed | tf_op | source)
XLA Modules:
  0.0 45.0 jit_solution(4319998171452339445)
XLA Ops:
  0.0 0.0 copy-start
  0.0 1.6 %copy-done = bf16[4,1024,256]{2,1,0:T(8,128)(2,1)S(1)} copy-done((bf16[4,1024,256]{2,1,0:T(8,128)(2,1)S(1)}, bf16[4,1024,256]{2,1,0:T(8,128)(2,1)}, u32[]{:S(2)}) %copy-start) | copy-done | bytes 2097176
  1.6 0.0 copy-start.1
  1.6 1.6 %copy-done.1 = bf16[4,1024,256]{2,1,0:T(8,128)(2,1)S(1)} copy-done((bf16[4,1024,256]{2,1,0:T(8,128)(2,1)S(1)}, bf16[4,1024,256]{2,1,0:T(8,128)(2,1)}, u32[]{:S(2)}) %copy-start.1) | copy-done | bytes 2097176
  3.2 0.0 copy-start.2
  3.2 1.0 %copy-done.2 = s32[16,8,1024]{2,1,0:T(8,128)S(1)} copy-done((s32[16,8,1024]{2,1,0:T(8,128)S(1)}, s32[16,8,1024]{2,1,0:T(8,128)}, u32[]{:S(2)}) %copy-start.2) | copy-done | bytes 524312
  4.2 0.0 copy-start.3
  4.2 1.0 %copy-done.3 = f32[16,8,1024]{2,1,0:T(8,128)S(1)} copy-done((f32[16,8,1024]{2,1,0:T(8,128)S(1)}, f32[16,8,1024]{2,1,0:T(8,128)}, u32[]{:S(2)}) %copy-start.3) | copy-done | bytes 524312
  5.3 0.0 copy-start.4
  5.3 0.9 %copy-done.4 = f32[8,64,128]{2,1,0:T(8,128)S(1)} copy-done((f32[8,64,128]{2,1,0:T(8,128)S(1)}, f32[8,64,128]{2,1,0:T(8,128)}, u32[]{:S(2)}) %copy-start.4) | copy-done | bytes 262168
  6.2 0.0 copy-start.5
  6.2 0.8 %copy-done.5 = f32[64,128]{1,0:T(8,128)S(1)} copy-done((f32[64,128]{1,0:T(8,128)S(1)}, f32[64,128]{1,0:T(8,128)}, u32[]{:S(2)}) %copy-start.5) | copy-done | bytes 32792
  7.0 0.0 copy-start.6
  7.0 0.8 %copy-done.6 = bf16[64,192]{1,0:T(8,128)(2,1)S(1)} copy-done((bf16[64,192]{1,0:T(8,128)(2,1)S(1)}, bf16[64,192]{1,0:T(8,128)(2,1)}, u32[]{:S(2)}) %copy-start.6) | copy-done | bytes 24600
  7.7 0.0 copy-start.7
  7.7 0.7 %copy-done.7 = s32[32]{0:T(128)S(1)} copy-done((s32[32]{0:T(128)S(1)}, s32[32]{0:T(128)}, u32[]{:S(2)}) %copy-start.7) | copy-done | bytes 152
  8.4 35.7 %shard_map.82 = f32[16,8,1024]{2,1,0:T(8,128)S(1)} custom-call(f32[16,8,1024]{2,1,0:T(8,128)S(1)} %copy-done.3, s32[16,8,1024]{2,1,0:T(8,128)S(1)} %copy-done.2, s32[1,32]{1,0:T(1,128)S(1)} %bitcast.1, bf16[4,1024,256]{2,1,0:T(8,128)(2,1)S(1)} %copy-done.1, bf16[4,1024,256]{2,1,0:T(8,128)(2,1)S(1)} %copy-done, bf16[64,192]{1,0:T(8,128)(2,1)S(1)} %copy-done.6, ...), custom_call_target="tpu_custom_call" | custom-call | flops 1610612736 | bytes 6291456 | tf_op jit(solution)/shard_map/pallas_call | solution.py:469
  44.1 0.9 %multiply_multiply_fusion = f32[16,8,1024]{2,1,0:T(8,128)} fusion(f32[16,8,1024]{2,1,0:T(8,128)S(1)} %shard_map.82, s32[16,8,1024]{2,1,0:T(8,128)S(1)} %copy-done.2), kind=kLoop, calls=%fused_computation | loop fusion | flops 655360 | bytes 1572864 | tf_op jit(solution)/shard_map/mul | solution.py:517
Async XLA Ops:
  0.0 1.6 %copy-start = (bf16[4,1024,256]{2,1,0:T(8,128)(2,1)S(1)}, bf16[4,1024,256]{2,1,0:T(8,128)(2,1)}, u32[]{:S(2)}) copy-start(bf16[4,1024,256]{2,1,0:T(8,128)(2,1)} %constant.17.clone.table_low) | copy-start | bytes 6291460
  1.6 1.6 %copy-start.1 = (bf16[4,1024,256]{2,1,0:T(8,128)(2,1)S(1)}, bf16[4,1024,256]{2,1,0:T(8,128)(2,1)}, u32[]{:S(2)}) copy-start(bf16[4,1024,256]{2,1,0:T(8,128)(2,1)} %constant.16.clone.table_high) | copy-start | bytes 6291460
  3.2 1.0 %copy-start.2 = (s32[16,8,1024]{2,1,0:T(8,128)S(1)}, s32[16,8,1024]{2,1,0:T(8,128)}, u32[]{:S(2)}) copy-start(s32[16,8,1024]{2,1,0:T(8,128)} %bins.1) | copy-start | bytes 1572868
  4.2 1.0 %copy-start.3 = (f32[16,8,1024]{2,1,0:T(8,128)S(1)}, f32[16,8,1024]{2,1,0:T(8,128)}, u32[]{:S(2)}) copy-start(f32[16,8,1024]{2,1,0:T(8,128)} %residual.1) | copy-start | bytes 1572868
  5.3 0.9 %copy-start.4 = (f32[8,64,128]{2,1,0:T(8,128)S(1)}, f32[8,64,128]{2,1,0:T(8,128)}, u32[]{:S(2)}) copy-start(f32[8,64,128]{2,1,0:T(8,128)} %constant.19.clone.wave_x) | copy-start | bytes 786436
  6.2 0.8 %copy-start.5 = (f32[64,128]{1,0:T(8,128)S(1)}, f32[64,128]{1,0:T(8,128)}, u32[]{:S(2)}) copy-start(f32[64,128]{1,0:T(8,128)} %constant.20.clone.wave_y) | copy-start | bytes 98308
  7.0 0.8 %copy-start.6 = (bf16[64,192]{1,0:T(8,128)(2,1)S(1)}, bf16[64,192]{1,0:T(8,128)(2,1)}, u32[]{:S(2)}) copy-start(bf16[64,192]{1,0:T(8,128)(2,1)} %constant.18.clone.table_y) | copy-start | bytes 73732
  7.7 0.7 %copy-start.7 = (s32[32]{0:T(128)S(1)}, s32[32]{0:T(128)}, u32[]{:S(2)}) copy-start(s32[32]{0:T(128)} %param.10) | copy-start | bytes 388

commit v2 on v1

--- a/solution.py
+++ b/solution.py
@@ -199,6 +199,10 @@
     field,
     res_v,
     bins_v,
+    classes_v,
+    table_y_v,
+    wave_x_v,
+    wave_y_v,
     high_v,
     low_v,
     send_a,
@@ -228,6 +232,13 @@
     half = lax.axis_index("dep")
     order = pair_order(me // 2)
 
+    barrier = pltpu.get_barrier_semaphore()
+    for step in range(1, count):
+        pl.semaphore_signal(
+            barrier, inc=1, device_id={"hor": lax.rem(me + step, count)}, device_id_type=MESH
+        )
+    pl.semaphore_signal(barrier, inc=1, device_id={"dep": 1 - half}, device_id_type=MESH)
+
     loads = [
         pltpu.make_async_copy(residual, res_v, load_sem.at[0]),
         pltpu.make_async_copy(bins, bins_v, load_sem.at[1]),
@@ -243,13 +254,14 @@
         for load in both:
             load.start()
         table_loads.append(both)
-
-    barrier = pltpu.get_barrier_semaphore()
-    for step in range(1, count):
-        pl.semaphore_signal(
-            barrier, inc=1, device_id={"hor": lax.rem(me + step, count)}, device_id_type=MESH
-        )
-    pl.semaphore_signal(barrier, inc=1, device_id={"dep": 1 - half}, device_id_type=MESH)
+    late_loads = [
+        pltpu.make_async_copy(classes, classes_v, load_sem.at[2]),
+        pltpu.make_async_copy(table_y, table_y_v, load_sem.at[3]),
+        pltpu.make_async_copy(wave_x.at[me], wave_x_v, load_sem.at[4]),
+        pltpu.make_async_copy(wave_y, wave_y_v, load_sem.at[5]),
+    ]
+    for load in late_loads:
+        load.start()
 
     for load in loads:
         load.wait()
@@ -285,8 +297,10 @@
             send_forward(other).start()
     recv_a[me] = send_a[me]
 
+    for load in late_loads:
+        load.wait()
     for layer in range(2 * layers):
-        index = jnp.full((8, width), classes[0, layer], jnp.int32).astype(jnp.float32)
+        index = jnp.full((8, width), classes_v[0, layer], jnp.int32).astype(jnp.float32)
         weights[layer] = weight_base * jnp.exp(weight_step * index)
 
     def layer_of(place):
@@ -296,7 +310,7 @@
         here = half * layers + layer_of(place)
         return coupling_scale * weights[here] * weights[here + 1 - 2 * half]
 
-    wave = (damping + smoothing * (wave_y[...] + wave_x[me][None])).reshape(y_cells // 8, 8, width)
+    wave = (damping + smoothing * (wave_y_v[...] + wave_x_v[...][None]))
 
     def pivot_step(place, carried):
         excess_part = carried
@@ -338,7 +352,7 @@
     def transform_y(first, second):
         values = jnp.concatenate([first, second], axis=1)
         upper, lower = split_values(values)
-        return dot32(table_y[...], jnp.concatenate([upper, upper, lower], axis=0))
+        return dot32(table_y_v[...], jnp.concatenate([upper, upper, lower], axis=0))
 
     def spectrum_step(index, carried):
         first = recv_a[:, 2 * index].reshape(y_cells, width)
@@ -456,24 +470,27 @@
     high_y, low_y = split_table(y_cells)
     table_y = np.concatenate([high_y, low_y, high_y], axis=1)
     wave_x = 2.0 - 2.0 * np.cos(np.arange(x_cells) * (2.0 * math.pi / x_cells))
-    wave_x = np.broadcast_to(wave_x.reshape(count, 1, width), (count, 8, width))
-    wave_x = np.tile(wave_x, (1, y_cells // 8, 1)).astype(np.float32)
+    wave_x = np.broadcast_to(wave_x.reshape(count, 1, width), (count, 8, width)).astype(np.float32)
     wave_y = 2.0 - 2.0 * np.cos(np.arange(y_cells) * (2.0 * math.pi / y_cells))
     wave_y = np.broadcast_to(wave_y[:, None], (y_cells, width)).astype(np.float32)
+    wave_y = wave_y.reshape(y_cells // 8, 8, width)
     block = (count, layers, y_rows, width)
     column = (layers, y_cells // 8, 8, width)
     f32, dma = jnp.float32, pltpu.SemaphoreType.DMA
     hbm = pl.BlockSpec(memory_space=pl.ANY)
     vmem = pl.BlockSpec(memory_space=pltpu.VMEM)
-    smem = pl.BlockSpec(memory_space=pltpu.SMEM)
     field = pl.pallas_call(
         kernel,
         out_shape=jax.ShapeDtypeStruct(residual.shape, f32),
-        in_specs=[hbm, hbm, smem, hbm, hbm, vmem, vmem, vmem],
+        in_specs=[hbm] * 8,
         out_specs=vmem,
         scratch_shapes=[
             pltpu.VMEM(residual.shape, f32),
             pltpu.VMEM(residual.shape, jnp.int32),
+            pltpu.SMEM((1, 2 * layers), jnp.int32),
+            pltpu.VMEM(table_y.shape, jnp.bfloat16),
+            pltpu.VMEM((8, width), f32),
+            pltpu.VMEM((y_cells // 8, 8, width), f32),
             pltpu.VMEM(high.shape, jnp.bfloat16),
             pltpu.VMEM(low.shape, jnp.bfloat16),
             pltpu.VMEM(block, f32),
@@ -486,7 +503,7 @@
             pltpu.VMEM(column, f32),
             pltpu.VMEM((2,) + column[1:], f32),
             pltpu.VMEM((2,) + column[1:], f32),
-            dma((2,)),
+            dma((6,)),
             dma((count // 2,)),
             dma((count // 2,)),
             dma((count,)),
@@ -497,7 +514,7 @@
             dma((2,)),
         ],
         compiler_params=pltpu.CompilerParams(
-            collective_id=0, has_side_effects=True, vmem_limit_bytes=40 * 2**20
+            collective_id=0, has_side_effects=True, vmem_limit_bytes=64 * 2**20
         ),
         cost_estimate=pl.CostEstimate(
             flops=2 * 6 * layers * y_rows * x_cells * x_cells,

time: 45.5 us -> 37.8 us (0.83)
  local copies, waits for them, and re-layouts: 8.38 us -> 0 us
  other arithmetic: 0.95 us -> 2.12 us
    unnamed x16 -> x0, local copies, waits for them, and re-layouts: 8.38 us -> none
    mul x1, other arithmetic: 0.95 us -> 2.12 us  [kernel_body(): return focusing(focus_bins) * field * (1.0 / (x_cells * y_cells))]
where the time goes in v2:
time: 37.8 us; the launch traced here: 37.7 us
  Pallas kernels  35.6 us (94%)
  other arithmetic  2.12 us (6%)
    pallas_call x1, Pallas kernels, kernel_body(): pl.pallas_call(kernel, out_shape=jax.ShapeDtypeStruct(residual.shape, f32...  35.6 us
    mul x1, other arithmetic, kernel_body(): return focusing(focus_bins) * field * (1.0 / (x_cells * y_cells))  2.12 us

profile of v2, /device:TPU:0, one launch (start us, length us, event | category | flops | bytes accessed | tf_op | source)
XLA Modules:
  0.0 37.7 jit_solution(3733039440136984819)
XLA Ops:
  0.0 35.6 %shard_map.82 = f32[16,8,1024]{2,1,0:T(8,128)} custom-call(f32[16,8,1024]{2,1,0:T(8,128)} %residual.1, s32[16,8,1024]{2,1,0:T(8,128)} %bins.1, s32[1,32]{1,0:T(1,128)} %bitcast.1, bf16[4,1024,256]{2,1,0:T(8,128)(2,1)} %constant.16.clone.table_high, bf16[4,1024,256]{2,1,0:T(8,128)(2,1)} %constant.17.clone.table_low, bf16[64,192]{1,0:T(8,128)(2,1)} %constant.18.clone.table_y, ...), custom_call_target="tpu_custom_call" | custom-call | flops 1610612736 | bytes 6291456 | tf_op jit(solution)/shard_map/pallas_call | solution.py:482
  35.6 2.1 %multiply_multiply_fusion = f32[16,8,1024]{2,1,0:T(8,128)} fusion(f32[16,8,1024]{2,1,0:T(8,128)} %shard_map.82, s32[16,8,1024]{2,1,0:T(8,128)} %bins.1), kind=kLoop, calls=%fused_computation | loop fusion | flops 655360 | bytes 1572864 | tf_op jit(solution)/shard_map/mul | solution.py:534

commit v3 on v0

--- a/solution.py
+++ b/solution.py
@@ -1,8 +1,13 @@
+import functools
 import math
 
 import jax
 import jax.numpy as jnp
+import ml_dtypes
+import numpy as np
 from jax import lax
+from jax.experimental import pallas as pl
+from jax.experimental.pallas import tpu as pltpu
 from jax.sharding import PartitionSpec as P
 
 damping = 0.01
@@ -154,10 +159,481 @@
     result_field = jnp.einsum("bzcj,bjx->zcx", arranged, table_back, precision=highest)
     return focus_map * result_field / (x_cells * y_cells)
 
+MESH = pl.DeviceIdType.MESH
+
+
+def split_table(length):
+    position = np.arange(length)
+    angles = (position[:, None] * position[None, :] % length) * (2.0 * math.pi / length)
+    table = np.cos(angles) + np.sin(angles)
+    high = table.astype(ml_dtypes.bfloat16)
+    low = (table - high.astype(np.float64)).astype(ml_dtypes.bfloat16)
+    return high, low
+
+
+def split_values(values):
+    high = values.astype(jnp.bfloat16)
+    low = (values - high.astype(jnp.float32)).astype(jnp.bfloat16)
+    return high, low
+
+
+def dot32(left, right):
+    return jnp.dot(left, right, preferred_element_type=jnp.float32)
+
+
+def kernel(
+    residual,
+    bins,
+    classes,
+    table_high,
+    table_low,
+    back_high,
+    back_low,
+    table_y,
+    wave_x,
+    wave_y,
+    result,
+    res_v,
+    bins_v,
+    classes_v,
+    table_y_v,
+    wave_x_v,
+    wave_y_v,
+    high_v,
+    low_v,
+    back_high_v,
+    back_low_v,
+    focus_v,
+    field_v,
+    send_a,
+    recv_a,
+    send_b,
+    recv_b,
+    weights,
+    inverse,
+    factor,
+    packed_inverse,
+    packed_factor,
+    spectrum,
+    upper_part,
+    gain_here,
+    gain_there,
+    edge_out,
+    edge_in,
+    load_sem,
+    table_sem,
+    send_a_sem,
+    recv_a_sem,
+    send_b_sem,
+    recv_b_sem,
+    edge_send_sem,
+    edge_recv_sem,
+    out_sem,
+):
+    _, count, pairs, y_rows, width = send_a.shape
+    layers = 2 * pairs
+    y_cells = count * y_rows
+    plane = (y_cells // 8, 8, width)
+    rows = layers * y_rows
+    me = lax.axis_index("hor")
+    half = lax.axis_index("dep")
+    near = me // 4
+    far = 1 - near
+
+    barrier = pltpu.get_barrier_semaphore()
+    for step in range(1, count):
+        pl.semaphore_signal(
+            barrier, inc=1, device_id={"hor": lax.rem(me + step, count)}, device_id_type=MESH
+        )
+    pl.semaphore_signal(barrier, inc=1, device_id={"dep": 1 - half}, device_id_type=MESH)
+
+    def table_copy(kind, block):
+        source = (table_high, table_low, back_high, back_low)[kind]
+        target = (high_v, low_v, back_high_v, back_low_v)[kind]
+        return pltpu.make_async_copy(
+            source.at[block], target.at[block], table_sem.at[kind, block]
+        )
+
+    loads = [
+        pltpu.make_async_copy(residual, res_v, load_sem.at[0]),
+        pltpu.make_async_copy(bins, bins_v, load_sem.at[1]),
+    ]
+    late_loads = [
+        pltpu.make_async_copy(classes, classes_v, load_sem.at[2]),
+        pltpu.make_async_copy(table_y, table_y_v, load_sem.at[3]),
+        pltpu.make_async_copy(wave_x.at[me], wave_x_v, load_sem.at[4]),
+        pltpu.make_async_copy(wave_y, wave_y_v, load_sem.at[5]),
+    ]
+    blocks = [far, near, 2 + far, 2 + near]
+    for load in loads:
+        load.start()
+    for block in blocks:
+        table_copy(0, block).start()
+        table_copy(1, block).start()
+    for load in late_loads:
+        load.start()
+
+    lane = lax.broadcasted_iota(jnp.int32, (y_cells, width), 1)
+    low_lanes = lane < width // 2
+
+    def turn(value):
+        return pltpu.roll(value, width // 2, 1)
+
+    def mix(first, second):
+        return (
+            jnp.where(low_lanes, first, turn(second)),
+            jnp.where(low_lanes, turn(first), second),
+        )
+
+    for load in loads:
+        load.wait()
+    focus_map = focus_base * jnp.exp(focus_step * bins_v[...].astype(jnp.float32))
+    scaled = (focus_map * res_v[...]).reshape(rows, count * width)
+    focus_v[...] = focus_map * (1.0 / (count * width * y_cells))
+    high, low = split_values(scaled)
+    stacked = jnp.concatenate([high, low], axis=0)
+
+    def send_forward(chunk, target):
+        return pltpu.make_async_remote_copy(
+            src_ref=send_a.at[chunk, target],
+            dst_ref=recv_a.at[chunk, me],
+            send_sem=send_a_sem.at[chunk, target],
+            recv_sem=recv_a_sem.at[chunk, me],
+            device_id={"hor": target},
+            device_id_type=MESH,
+        )
+
+    def wait_forward(chunk, source):
+        pltpu.make_async_remote_copy(
+            src_ref=send_a.at[chunk, source],
+            dst_ref=recv_a.at[chunk, source],
+            send_sem=send_a_sem.at[chunk, source],
+            recv_sem=recv_a_sem.at[chunk, source],
+            device_id={"hor": source},
+            device_id_type=MESH,
+        ).wait_recv()
+
+    def send_back(chunk, target):
+        return pltpu.make_async_remote_copy(
+            src_ref=send_b.at[chunk, target],
+            dst_ref=recv_b.at[chunk, me],
+            send_sem=send_b_sem.at[chunk, target],
+            recv_sem=recv_b_sem.at[chunk, me],
+            device_id={"hor": target},
+            device_id_type=MESH,
+        )
+
+    def wait_back(chunk, source):
+        pltpu.make_async_remote_copy(
+            src_ref=send_b.at[chunk, source],
+            dst_ref=recv_b.at[chunk, source],
+            send_sem=send_b_sem.at[chunk, source],
+            recv_sem=recv_b_sem.at[chunk, source],
+            device_id={"hor": source},
+            device_id_type=MESH,
+        ).wait_recv()
+
+    far_targets = [4 * far + lax.rem(me + step, 4) for step in range(4)]
+    near_targets = [4 * near + lax.rem(me + step, 4) for step in range(1, 4)]
+    others = far_targets + near_targets
+
+    for step, block in enumerate(blocks):
+        chunk = step // 2
+        side = far if step % 2 == 0 else near
+        table_copy(0, block).wait()
+        table_copy(1, block).wait()
+        first = dot32(stacked, high_v[block])
+        value = first[:rows] + first[rows:] + dot32(high, low_v[block])
+        for pair in range(2):
+            part = value[:, pair * width : (pair + 1) * width]
+            even, odd = mix(part[: rows // 2], part[rows // 2 :])
+            send_a[chunk, 4 * side + 2 * pair] = even.reshape(pairs, y_rows, width)
+            send_a[chunk, 4 * side + 2 * pair + 1] = odd.reshape(pairs, y_rows, width)
+        if step == 0:
+            pl.semaphore_wait(barrier, count)
+        for target in far_targets if step % 2 == 0 else near_targets:
+            send_forward(chunk, target).start()
+        if step % 2 == 1:
+            recv_a[chunk, me] = send_a[chunk, me]
+
+    for kind in (2, 3):
+        for block in range(4):
+            table_copy(kind, block).start()
+
+    for load in late_loads:
+        load.wait()
+    for layer in range(2 * layers):
+        index = jnp.full((8, width), classes_v[0, layer], jnp.int32).astype(jnp.float32)
+        weights[layer] = weight_base * jnp.exp(weight_step * index)
+
+    def layer_of(place):
+        return place + half * (layers - 1 - 2 * place)
+
+    def coupling_after(place):
+        here = half * layers + layer_of(place)
+        return coupling_scale * weights[here] * weights[here + 1 - 2 * half]
+
+    wave = damping + smoothing * (wave_y_v[...] + wave_x_v[...][None])
+
+    def pivot_step(place, carried):
+        here = weights[half * layers + layer_of(place)]
+        excess = here[None] * wave + carried
+        after = coupling_after(place)[None]
+        reciprocal = 1.0 / (excess + after)
+        inverse[layer_of(place)] = reciprocal
+        scaled_after = after * reciprocal
+        factor[layer_of(place)] = scaled_after
+        edge_out[0] = excess
+        return scaled_after * excess
+
+    lax.fori_loop(0, layers, pivot_step, jnp.zeros(plane, jnp.float32))
+
+    def edge_copy(slot):
+        return pltpu.make_async_remote_copy(
+            src_ref=edge_out.at[slot],
+            dst_ref=edge_in.at[slot],
+            send_sem=edge_send_sem.at[slot],
+            recv_sem=edge_recv_sem.at[slot],
+            device_id={"dep": 1 - half},
+            device_id_type=MESH,
+        )
+
+    edge_copy(0).start()
+
+    def flat(value):
+        return value.reshape(y_cells, width)
+
+    def pack_step(row, carried):
+        parts = mix(flat(inverse[row]), flat(inverse[row + pairs]))
+        packed_inverse[0, row], packed_inverse[1, row] = (part.reshape(plane) for part in parts)
+        parts = mix(flat(factor[row]), flat(factor[row + pairs]))
+        packed_factor[0, row], packed_factor[1, row] = (part.reshape(plane) for part in parts)
+        return carried
+
+    lax.fori_loop(0, pairs, pack_step, 0)
+
+    edge_copy(0).wait()
+    after = coupling_after(layers - 1)[None]
+    here = edge_out[0]
+    there = edge_in[0]
+    scale = 1.0 / (here * there + after * (here + there))
+    for target, value in ((gain_here, (there + after) * scale), (gain_there, after * scale)):
+        parts = mix(flat(value), flat(value))
+        target[0], target[1] = (part.reshape(plane) for part in parts)
+
+    low_plane = low_lanes.reshape(plane)
+    first_lanes = jnp.logical_xor(low_plane, jnp.full(plane, half, jnp.int32) == 1)
+
+    def turn_plane(value):
+        return turn(flat(value)).reshape(plane)
+
+    def row_of(place):
+        return place + half * (pairs - 1 - 2 * place)
+
+    def transform_y(first, second):
+        upper, lower = split_values(jnp.concatenate([first, second], axis=1))
+        return dot32(table_y_v[...], jnp.concatenate([upper, upper, lower], axis=0))
+
+    for chunk in range(2):
+        for source in others:
+            wait_forward(chunk, source)
+        for row in range(0, pairs, 2):
+            value = transform_y(flat(recv_a[chunk, :, row]), flat(recv_a[chunk, :, row + 1]))
+            spectrum[row] = value[:, :width].reshape(plane)
+            spectrum[row + 1] = value[:, width:].reshape(plane)
+        carried = jnp.zeros(plane, jnp.float32)
+        for side in range(2):
+            for place in range(pairs):
+                row = row_of(place)
+                value = spectrum[row] + carried
+                spectrum[row] = value
+                forwarded = packed_factor[chunk, row] * value
+                carried = jnp.where(first_lanes, forwarded, 0.0)
+                if side == 1:
+                    carried = forwarded - carried
+            carried = turn_plane(carried)
+        edge_out[1 + chunk] = value
+        edge_copy(1 + chunk).start()
+        edge_copy(1 + chunk).wait()
+        following = gain_here[chunk] * value + gain_there[chunk] * turn_plane(edge_in[1 + chunk])
+        upper_part[row_of(pairs - 1)] = following
+        for place in reversed(range(pairs - 1)):
+            row = row_of(place)
+            following = (
+                packed_inverse[chunk, row] * spectrum[row] + packed_factor[chunk, row] * following
+            )
+            upper_part[row] = following
+        following = turn_plane(following)
+        for place in reversed(range(pairs)):
+            row = row_of(place)
+            following = (
+                packed_inverse[chunk, row] * spectrum[row] + packed_factor[chunk, row] * following
+            )
+            spectrum[row] = jnp.where(first_lanes, following, upper_part[row])
+        for row in range(0, pairs, 2):
+            value = transform_y(flat(spectrum[row]), flat(spectrum[row + 1]))
+            send_b[chunk, :, row] = value[:, :width].reshape(count, y_rows, width)
+            send_b[chunk, :, row + 1] = value[:, width:].reshape(count, y_rows, width)
+        for target in others:
+            send_back(chunk, target).start()
+        recv_b[chunk, me] = send_b[chunk, me]
+
+    for kind in (2, 3):
+        for block in range(4):
+            table_copy(kind, block).wait()
+
+    def gathered(chunk, side):
+        tops = []
+        bottoms = []
+        for pair in range(2):
+            even = flat(recv_b[chunk, 4 * side + 2 * pair])
+            odd = flat(recv_b[chunk, 4 * side + 2 * pair + 1])
+            top, bottom = mix(even, odd)
+            tops.append(top)
+            bottoms.append(bottom)
+        value = jnp.concatenate(
+            [jnp.concatenate(tops, axis=1), jnp.concatenate(bottoms, axis=1)], axis=0
+        )
+        upper, lower = split_values(value)
+        return jnp.concatenate([upper, lower], axis=0), upper
+
+    def product(stacked, upper, block, columns):
+        first = dot32(stacked, back_high_v[block, :, columns])
+        return first[:rows] + first[rows:] + dot32(upper, back_low_v[block, :, columns])
+
+    def out_copy(index):
+        columns = pl.ds(index * 2 * width, 2 * width)
+        return pltpu.make_async_copy(
+            field_v.at[:, :, columns], result.at[:, :, columns], out_sem.at[index]
+        )
+
+    for step in range(4):
+        chunk = step // 2
+        side = near if step % 2 == 0 else far
+        for source in near_targets if step % 2 == 0 else far_targets:
+            wait_back(chunk, source)
+        pieces = gathered(chunk, side)
+        for index in range(count // 2):
+            columns = slice(index * 2 * width, (index + 1) * 2 * width)
+            total = product(*pieces, 2 * chunk + side, columns).reshape(layers, y_rows, 2 * width)
+            if step > 0:
+                total = total + field_v[:, :, columns]
+            if step == 3:
+                total = total * focus_v[:, :, columns]
+            field_v[:, :, columns] = total
+            if step == 3:
+                out_copy(index).start()
+
+    for chunk in range(2):
+        for target in others:
+            send_forward(chunk, target).wait_send()
+            send_back(chunk, target).wait_send()
+    for index in range(count // 2):
+        out_copy(index).wait()
+
+
+def kernel_body(residual, focus_bins, layer_class):
+    layers, y_rows, x_cells = residual.shape
+    count = lax.axis_size("hor")
+    width = x_cells // count
+    y_cells = y_rows * count
+    forward = []
+    backward = []
+    for table in split_table(x_cells):
+        table = table.reshape(x_cells, count, 2, width // 2).transpose(2, 1, 3, 0)
+        table = np.ascontiguousarray(table.reshape(4, 2 * width, x_cells))
+        backward.append(table)
+        forward.append(np.ascontiguousarray(table.transpose(0, 2, 1)))
+    high_y, low_y = split_table(y_cells)
+    table_y = np.concatenate([high_y, low_y, high_y], axis=1)
+    wave_x = 2.0 - 2.0 * np.cos(np.arange(x_cells) * (2.0 * math.pi / x_cells))
+    wave_x = np.broadcast_to(wave_x.reshape(count, 1, width), (count, 8, width)).astype(np.float32)
+    wave_y = 2.0 - 2.0 * np.cos(np.arange(y_cells) * (2.0 * math.pi / y_cells))
+    wave_y = np.broadcast_to(wave_y[:, None], (y_cells, width)).astype(np.float32)
+    wave_y = wave_y.reshape(y_cells // 8, 8, width)
+    pairs = layers // 2
+    block = (2, count, pairs, y_rows, width)
+    plane = (y_cells // 8, 8, width)
+    f32, bf16, dma = jnp.float32, jnp.bfloat16, pltpu.SemaphoreType.DMA
+    return pl.pallas_call(
+        kernel,
+        out_shape=jax.ShapeDtypeStruct(residual.shape, f32),
+        in_specs=[pl.BlockSpec(memory_space=pl.ANY)] * 10,
+        out_specs=pl.BlockSpec(memory_space=pl.ANY),
+        scratch_shapes=[
+            pltpu.VMEM(residual.shape, f32),
+            pltpu.VMEM(residual.shape, jnp.int32),
+            pltpu.SMEM((1, 2 * layers), jnp.int32),
+            pltpu.VMEM(table_y.shape, bf16),
+            pltpu.VMEM((8, width), f32),
+            pltpu.VMEM(plane, f32),
+            pltpu.VMEM(forward[0].shape, bf16),
+            pltpu.VMEM(forward[1].shape, bf16),
+            pltpu.VMEM(backward[0].shape, bf16),
+            pltpu.VMEM(backward[1].shape, bf16),
+            pltpu.VMEM(residual.shape, f32),
+            pltpu.VMEM(residual.shape, f32),
+            pltpu.VMEM(block, f32),
+            pltpu.VMEM(block, f32),
+            pltpu.VMEM(block, f32),
+            pltpu.VMEM(block, f32),
+            pltpu.VMEM((2 * layers, 8, width), f32),
+            pltpu.VMEM((layers,) + plane, f32),
+            pltpu.VMEM((layers,) + plane, f32),
+            pltpu.VMEM((2, pairs) + plane, f32),
+            pltpu.VMEM((2, pairs) + plane, f32),
+            pltpu.VMEM((pairs,) + plane, f32),
+            pltpu.VMEM((pairs,) + plane, f32),
+            pltpu.VMEM((2,) + plane, f32),
+            pltpu.VMEM((2,) + plane, f32),
+            pltpu.VMEM((3,) + plane, f32),
+            pltpu.VMEM((3,) + plane, f32),
+            dma((6,)),
+            dma((4, 4)),
+            dma((2, count)),
+            dma((2, count)),
+            dma((2, count)),
+            dma((2, count)),
+            dma((3,)),
+            dma((3,)),
+            dma((count // 2,)),
+        ],
+        compiler_params=pltpu.CompilerParams(
+            collective_id=0, has_side_effects=True, vmem_limit_bytes=64 * 2**20
+        ),
+        cost_estimate=pl.CostEstimate(
+            flops=2 * 6 * layers * y_rows * x_cells * x_cells,
+            bytes_accessed=10 * 2**20,
+            transcendentals=layers * y_rows * x_cells,
+        ),
+    )(
+        residual,
+        focus_bins,
+        layer_class.reshape(1, -1),
+        jnp.asarray(forward[0]),
+        jnp.asarray(forward[1]),
+        jnp.asarray(backward[0]),
+        jnp.asarray(backward[1]),
+        jnp.asarray(table_y),
+        jnp.asarray(wave_x),
+        jnp.asarray(wave_y),
+    )
+
+
+def fits_kernel(mesh):
+    return mesh.shape["hor"] == 8 and mesh.shape["dep"] == 2
+
+
+def chosen(mesh, residual, focus_bins, layer_class):
+    shape = residual.shape
+    if fits_kernel(mesh) and shape == (16, 8, 1024):
+        return kernel_body(residual, focus_bins, layer_class)
+    return body(residual, focus_bins, layer_class)
+
 
 def solution(mesh):
     return jax.shard_map(
-        body,
+        functools.partial(chosen, mesh),
         mesh=mesh,
         in_specs=(P(("grp", "dep"), "hor", None), P(("grp", "dep"), "hor", None), P("grp")),
         out_specs=P(("grp", "dep"), "hor", None),

time: 96.1 us -> 35.5 us (0.37)
  matrix products: 44.3 us -> 0 us
  Pallas kernels: 0 us -> 33.5 us
  blocking collectives: 18.4 us -> 0 us
  waiting for transfers between devices: 9.43 us -> 0 us
  starting transfers between devices: 7.35 us -> 0 us
  local copies, waits for them, and re-layouts: 9.11 us -> 1.89 us
  other arithmetic: 6.73 us -> 0 us
    dot_general x4 -> x0, matrix products: 44.3 us -> none  [the longest x1 20.2 us: body(): jnp.einsum('zcx,xbj->bzcj', scaled, table_x.reshape(x_cells, hor_count, b...]
    pallas_call x0 -> x1, Pallas kernels: none -> 33.5 us  [kernel_body(): pl.pallas_call(kernel, out_shape=jax.ShapeDtypeStruct(residual.shape, f32...]
    all_to_all x1 -> x0, blocking collectives: 18.4 us -> none  [body(): lax.all_to_all(returned, 'hor', split_axis=0, concat_axis=0, tiled=True)]
    all_to_all x1 -> x0, waiting for transfers between devices: 8.19 us -> none  [body(): lax.all_to_all(spectra, 'hor', split_axis=0, concat_axis=0, tiled=True)]
    all_to_all x1 -> x0, starting transfers between devices: 7.28 us -> none  [body(): lax.all_to_all(spectra, 'hor', split_axis=0, concat_axis=0, tiled=True)]
    add x13 -> x0, other arithmetic: 3.72 us -> none  [the longest x4 1.78 us: reduce_step(): new_middle = middle + ratio_below * upper_below + ratio_above * lower_above]
    mul x11 -> x0, other arithmetic: 2.25 us -> none  [the longest x1 1.31 us: body(): scaled = focus_map * residual]
    unnamed x16 -> x1, local copies, waits for them, and re-layouts: 3.92 us -> 1.89 us
  transfers between devices with their start and end apart: 2 -> 0, of which waited for: 2 -> 0; matrix products, arithmetic and copies ran while one was open for 6% -> 0% of each run, Pallas kernels for 0% -> 0%
where the time goes in v3:
time: 35.5 us; the launch traced here: 35.4 us
  Pallas kernels  33.5 us (94%)
  local copies, waits for them, and re-layouts  1.89 us (5%)
    pallas_call x1, Pallas kernels, kernel_body(): pl.pallas_call(kernel, out_shape=jax.ShapeDtypeStruct(residual.shape, f32...  33.5 us
    unnamed x1, local copies, waits for them, and re-layouts  1.89 us

profile of v3, /device:TPU:0, one launch (start us, length us, event | category | flops | bytes accessed | tf_op | source)
XLA Modules:
  0.0 35.4 jit_solution(12755205569297800928)
XLA Ops:
  0.0 33.5 %shard_map.100 = f32[16,8,1024]{2,1,0:T(8,128)} custom-call(f32[16,8,1024]{2,1,0:T(8,128)} %residual.1, s32[16,8,1024]{2,1,0:T(8,128)} %bins.1, s32[1,32]{1,0:T(1,128)} %bitcast.1, bf16[4,1024,256]{2,1,0:T(8,128)(2,1)} %constant.14.clone.table_high, bf16[4,1024,256]{2,1,0:T(8,128)(2,1)} %constant.15.clone.table_low, ...), custom_call_target="tpu_custom_call" | custom-call | flops 1610612736 | bytes 10485760 | tf_op jit(solution)/shard_map/pallas_call | solution.py:558
  33.5 1.9 %copy.12 = f32[16,8,1024]{2,1,0:T(8,128)} copy(f32[16,8,1024]{2,1,0:T(8,128)} %shard_map.100) | data formatting | bytes 1048576

commit v4 on v3

--- a/solution.py
+++ b/solution.py
@@ -351,8 +351,9 @@
             send_a[chunk, 4 * side + 2 * pair + 1] = odd.reshape(pairs, y_rows, width)
         if step == 0:
             pl.semaphore_wait(barrier, count)
-        for target in far_targets if step % 2 == 0 else near_targets:
-            send_forward(chunk, target).start()
+        if chunk == 0:
+            for target in far_targets if step == 0 else near_targets:
+                send_forward(0, target).start()
         if step % 2 == 1:
             recv_a[chunk, me] = send_a[chunk, me]
 
@@ -420,6 +421,10 @@
     for target, value in ((gain_here, (there + after) * scale), (gain_there, after * scale)):
         parts = mix(flat(value), flat(value))
         target[0], target[1] = (part.reshape(plane) for part in parts)
+
+    for target in others:
+        send_forward(0, target).wait_send()
+        send_forward(1, target).start()
 
     low_plane = low_lanes.reshape(plane)
     first_lanes = jnp.logical_xor(low_plane, jnp.full(plane, half, jnp.int32) == 1)
@@ -526,7 +531,8 @@
 
     for chunk in range(2):
         for target in others:
-            send_forward(chunk, target).wait_send()
+            if chunk == 1:
+                send_forward(1, target).wait_send()
             send_back(chunk, target).wait_send()
     for index in range(count // 2):
         out_copy(index).wait()

time: 35.5 us -> 34.7 us (0.977)
  Pallas kernels: 33.5 us -> 32.6 us
    pallas_call x1, Pallas kernels: 33.5 us -> 32.6 us  [kernel_body(): pl.pallas_call(kernel, out_shape=jax.ShapeDtypeStruct(residual.shape, f32...]
where the time goes in v4:
time: 34.7 us; the launch traced here: 34.5 us
  Pallas kernels  32.6 us (94%)
  local copies, waits for them, and re-layouts  1.89 us (5%)
    pallas_call x1, Pallas kernels, kernel_body(): pl.pallas_call(kernel, out_shape=jax.ShapeDtypeStruct(residual.shape, f32...  32.6 us
    unnamed x1, local copies, waits for them, and re-layouts  1.89 us

profile of v4, /device:TPU:0, one launch (start us, length us, event | category | flops | bytes accessed | tf_op | source)
XLA Modules:
  0.0 34.5 jit_solution(5509669816570833809)
XLA Ops:
  0.0 32.6 %shard_map.100 = f32[16,8,1024]{2,1,0:T(8,128)} custom-call(f32[16,8,1024]{2,1,0:T(8,128)} %residual.1, s32[16,8,1024]{2,1,0:T(8,128)} %bins.1, s32[1,32]{1,0:T(1,128)} %bitcast.1, bf16[4,1024,256]{2,1,0:T(8,128)(2,1)} %constant.14.clone.table_high, bf16[4,1024,256]{2,1,0:T(8,128)(2,1)} %constant.15.clone.table_low, ...), custom_call_target="tpu_custom_call" | custom-call | flops 1610612736 | bytes 10485760 | tf_op jit(solution)/shard_map/pallas_call | solution.py:564
  32.6 1.9 %copy.12 = f32[16,8,1024]{2,1,0:T(8,128)} copy(f32[16,8,1024]{2,1,0:T(8,128)} %shard_map.100) | data formatting | bytes 1048576

commit v5 on v4

--- a/solution.py
+++ b/solution.py
@@ -189,22 +189,16 @@
     table_low,
     back_high,
     back_low,
-    table_y,
-    wave_x,
-    wave_y,
     result,
     res_v,
     bins_v,
     classes_v,
     table_y_v,
-    wave_x_v,
-    wave_y_v,
     high_v,
     low_v,
     back_high_v,
     back_low_v,
     focus_v,
-    field_v,
     send_a,
     recv_a,
     send_b,
@@ -214,6 +208,8 @@
     factor,
     packed_inverse,
     packed_factor,
+    response,
+    packed_response,
     spectrum,
     upper_part,
     gain_here,
@@ -228,12 +224,12 @@
     recv_b_sem,
     edge_send_sem,
     edge_recv_sem,
-    out_sem,
 ):
     _, count, pairs, y_rows, width = send_a.shape
     layers = 2 * pairs
     y_cells = count * y_rows
     plane = (y_cells // 8, 8, width)
+    x_cells = count * width
     rows = layers * y_rows
     me = lax.axis_index("hor")
     half = lax.axis_index("dep")
@@ -251,7 +247,9 @@
         source = (table_high, table_low, back_high, back_low)[kind]
         target = (high_v, low_v, back_high_v, back_low_v)[kind]
         return pltpu.make_async_copy(
-            source.at[block], target.at[block], table_sem.at[kind, block]
+            source.at[block, pl.ds(0, target.shape[1])],
+            target.at[block],
+            table_sem.at[kind, block],
         )
 
     loads = [
@@ -260,9 +258,9 @@
     ]
     late_loads = [
         pltpu.make_async_copy(classes, classes_v, load_sem.at[2]),
-        pltpu.make_async_copy(table_y, table_y_v, load_sem.at[3]),
-        pltpu.make_async_copy(wave_x.at[me], wave_x_v, load_sem.at[4]),
-        pltpu.make_async_copy(wave_y, wave_y_v, load_sem.at[5]),
+        pltpu.make_async_copy(
+            table_high.at[0, pl.ds(x_cells, y_cells)], table_y_v, load_sem.at[3]
+        ),
     ]
     blocks = [far, near, 2 + far, 2 + near]
     for load in loads:
@@ -374,7 +372,14 @@
         here = half * layers + layer_of(place)
         return coupling_scale * weights[here] * weights[here + 1 - 2 * half]
 
-    wave = damping + smoothing * (wave_y_v[...] + wave_x_v[...][None])
+    def half_sines(frequency, length):
+        sines = jnp.sin(frequency.astype(jnp.float32) * (math.pi / length))
+        return 4.0 * sines * sines
+
+    wave_x = half_sines(lax.broadcasted_iota(jnp.int32, (8, width), 1) + me * width, x_cells)
+    row_index = lax.broadcasted_iota(jnp.int32, (y_cells, width), 0)
+    wave_y = half_sines(row_index, y_cells).reshape(plane)
+    wave = damping + smoothing * (wave_y + wave_x[None])
 
     def pivot_step(place, carried):
         here = weights[half * layers + layer_of(place)]
@@ -401,6 +406,16 @@
 
     edge_copy(0).start()
 
+    def response_step(step, following):
+        place = layers - 2 - step
+        value = factor[layer_of(place)] * following
+        response[layer_of(place)] = value
+        return value
+
+    ones = jnp.ones(plane, jnp.float32)
+    response[layer_of(layers - 1)] = ones
+    lax.fori_loop(0, layers - 1, response_step, ones)
+
     def flat(value):
         return value.reshape(y_cells, width)
 
@@ -409,6 +424,8 @@
         packed_inverse[0, row], packed_inverse[1, row] = (part.reshape(plane) for part in parts)
         parts = mix(flat(factor[row]), flat(factor[row + pairs]))
         packed_factor[0, row], packed_factor[1, row] = (part.reshape(plane) for part in parts)
+        parts = mix(flat(response[row]), flat(response[row + pairs]))
+        packed_response[0, row], packed_response[1, row] = (part.reshape(plane) for part in parts)
         return carried
 
     lax.fori_loop(0, pairs, pack_step, 0)
@@ -437,7 +454,7 @@
 
     def transform_y(first, second):
         upper, lower = split_values(jnp.concatenate([first, second], axis=1))
-        return dot32(table_y_v[...], jnp.concatenate([upper, upper, lower], axis=0))
+        return dot32(table_y_v[...], jnp.concatenate([upper, upper, lower, lower], axis=0))
 
     for chunk in range(2):
         for source in others:
@@ -459,8 +476,7 @@
             carried = turn_plane(carried)
         edge_out[1 + chunk] = value
         edge_copy(1 + chunk).start()
-        edge_copy(1 + chunk).wait()
-        following = gain_here[chunk] * value + gain_there[chunk] * turn_plane(edge_in[1 + chunk])
+        following = jnp.zeros(plane, jnp.float32)
         upper_part[row_of(pairs - 1)] = following
         for place in reversed(range(pairs - 1)):
             row = row_of(place)
@@ -475,8 +491,13 @@
                 packed_inverse[chunk, row] * spectrum[row] + packed_factor[chunk, row] * following
             )
             spectrum[row] = jnp.where(first_lanes, following, upper_part[row])
+        edge_copy(1 + chunk).wait()
+        edge = gain_here[chunk] * value + gain_there[chunk] * turn_plane(edge_in[1 + chunk])
+        edge = jnp.where(first_lanes, turn_plane(edge), edge)
         for row in range(0, pairs, 2):
-            value = transform_y(flat(spectrum[row]), flat(spectrum[row + 1]))
+            first = spectrum[row] + packed_response[chunk, row] * edge
+            second = spectrum[row + 1] + packed_response[chunk, row + 1] * edge
+            value = transform_y(flat(first), flat(second))
             send_b[chunk, :, row] = value[:, :width].reshape(count, y_rows, width)
             send_b[chunk, :, row + 1] = value[:, width:].reshape(count, y_rows, width)
         for target in others:
@@ -506,12 +527,6 @@
         first = dot32(stacked, back_high_v[block, :, columns])
         return first[:rows] + first[rows:] + dot32(upper, back_low_v[block, :, columns])
 
-    def out_copy(index):
-        columns = pl.ds(index * 2 * width, 2 * width)
-        return pltpu.make_async_copy(
-            field_v.at[:, :, columns], result.at[:, :, columns], out_sem.at[index]
-        )
-
     for step in range(4):
         chunk = step // 2
         side = near if step % 2 == 0 else far
@@ -522,20 +537,16 @@
             columns = slice(index * 2 * width, (index + 1) * 2 * width)
             total = product(*pieces, 2 * chunk + side, columns).reshape(layers, y_rows, 2 * width)
             if step > 0:
-                total = total + field_v[:, :, columns]
+                total = total + result[:, :, columns]
             if step == 3:
                 total = total * focus_v[:, :, columns]
-            field_v[:, :, columns] = total
-            if step == 3:
-                out_copy(index).start()
+            result[:, :, columns] = total
 
     for chunk in range(2):
         for target in others:
             if chunk == 1:
                 send_forward(1, target).wait_send()
             send_back(chunk, target).wait_send()
-    for index in range(count // 2):
-        out_copy(index).wait()
 
 
 def kernel_body(residual, focus_bins, layer_class):
@@ -551,12 +562,9 @@
         backward.append(table)
         forward.append(np.ascontiguousarray(table.transpose(0, 2, 1)))
     high_y, low_y = split_table(y_cells)
-    table_y = np.concatenate([high_y, low_y, high_y], axis=1)
-    wave_x = 2.0 - 2.0 * np.cos(np.arange(x_cells) * (2.0 * math.pi / x_cells))
-    wave_x = np.broadcast_to(wave_x.reshape(count, 1, width), (count, 8, width)).astype(np.float32)
-    wave_y = 2.0 - 2.0 * np.cos(np.arange(y_cells) * (2.0 * math.pi / y_cells))
-    wave_y = np.broadcast_to(wave_y[:, None], (y_cells, width)).astype(np.float32)
-    wave_y = wave_y.reshape(y_cells // 8, 8, width)
+    table_y = np.concatenate([high_y, low_y, high_y, low_y], axis=1)
+    filler = np.broadcast_to(table_y, (4,) + table_y.shape)
+    forward[0] = np.concatenate([forward[0], filler], axis=1)
     pairs = layers // 2
     block = (2, count, pairs, y_rows, width)
     plane = (y_cells // 8, 8, width)
@@ -564,20 +572,17 @@
     return pl.pallas_call(
         kernel,
         out_shape=jax.ShapeDtypeStruct(residual.shape, f32),
-        in_specs=[pl.BlockSpec(memory_space=pl.ANY)] * 10,
-        out_specs=pl.BlockSpec(memory_space=pl.ANY),
+        in_specs=[pl.BlockSpec(memory_space=pl.ANY)] * 7,
+        out_specs=pl.BlockSpec(memory_space=pltpu.VMEM),
         scratch_shapes=[
             pltpu.VMEM(residual.shape, f32),
             pltpu.VMEM(residual.shape, jnp.int32),
             pltpu.SMEM((1, 2 * layers), jnp.int32),
             pltpu.VMEM(table_y.shape, bf16),
-            pltpu.VMEM((8, width), f32),
-            pltpu.VMEM(plane, f32),
-            pltpu.VMEM(forward[0].shape, bf16),
+            pltpu.VMEM(forward[1].shape, bf16),
             pltpu.VMEM(forward[1].shape, bf16),
             pltpu.VMEM(backward[0].shape, bf16),
             pltpu.VMEM(backward[1].shape, bf16),
-            pltpu.VMEM(residual.shape, f32),
             pltpu.VMEM(residual.shape, f32),
             pltpu.VMEM(block, f32),
             pltpu.VMEM(block, f32),
@@ -588,13 +593,15 @@
             pltpu.VMEM((layers,) + plane, f32),
             pltpu.VMEM((2, pairs) + plane, f32),
             pltpu.VMEM((2, pairs) + plane, f32),
+            pltpu.VMEM((layers,) + plane, f32),
+            pltpu.VMEM((2, pairs) + plane, f32),
             pltpu.VMEM((pairs,) + plane, f32),
             pltpu.VMEM((pairs,) + plane, f32),
             pltpu.VMEM((2,) + plane, f32),
             pltpu.VMEM((2,) + plane, f32),
             pltpu.VMEM((3,) + plane, f32),
             pltpu.VMEM((3,) + plane, f32),
-            dma((6,)),
+            dma((4,)),
             dma((4, 4)),
             dma((2, count)),
             dma((2, count)),
@@ -602,10 +609,9 @@
             dma((2, count)),
             dma((3,)),
             dma((3,)),
-            dma((count // 2,)),
         ],
         compiler_params=pltpu.CompilerParams(
-            collective_id=0, has_side_effects=True, vmem_limit_bytes=64 * 2**20
+            collective_id=0, has_side_effects=True, vmem_limit_bytes=53 * 2**20
         ),
         cost_estimate=pl.CostEstimate(
             flops=2 * 6 * layers * y_rows * x_cells * x_cells,
@@ -620,9 +626,6 @@
         jnp.asarray(forward[1]),
         jnp.asarray(backward[0]),
         jnp.asarray(backward[1]),
-        jnp.asarray(table_y),
-        jnp.asarray(wave_x),
-        jnp.asarray(wave_y),
     )
 
 

time: 34.7 us -> 33.8 us (0.974)
  local copies, waits for them, and re-layouts: 1.89 us -> 1.45 us
  Pallas kernels: 32.6 us -> 32.2 us
    pallas_call x1, Pallas kernels: 32.6 us -> 32.2 us  [kernel_body(): pl.pallas_call(kernel, out_shape=jax.ShapeDtypeStruct(residual.shape, f32...]
    unnamed x1 -> x3, local copies, waits for them, and re-layouts: 1.89 us -> 1.45 us
where the time goes in v5:
time: 33.8 us; the launch traced here: 33.7 us
  Pallas kernels  32.2 us (95%)
  local copies, waits for them, and re-layouts  1.45 us (4%)
    pallas_call x1, Pallas kernels, kernel_body(): pl.pallas_call(kernel, out_shape=jax.ShapeDtypeStruct(residual.shape, f32...  32.2 us
    unnamed x3, local copies, waits for them, and re-layouts  1.45 us

profile of v5, /device:TPU:0, one launch (start us, length us, event | category | flops | bytes accessed | tf_op | source)
XLA Modules:
  0.0 33.7 jit_solution(11217320700687725587)
XLA Ops:
  0.0 0.0 copy-start
  0.0 0.7 %copy-done = s32[32]{0:T(128)S(1)} copy-done((s32[32]{0:T(128)S(1)}, s32[32]{0:T(128)}, u32[]{:S(2)}) %copy-start) | copy-done | bytes 152
  0.7 32.2 %shard_map.73 = f32[16,8,1024]{2,1,0:T(8,128)S(1)} custom-call(f32[16,8,1024]{2,1,0:T(8,128)} %residual.1, s32[16,8,1024]{2,1,0:T(8,128)} %bins.1, s32[1,32]{1,0:T(1,128)S(1)} %bitcast.1, bf16[4,1088,256]{2,1,0:T(8,128)(2,1)} %constant.8.clone.table_high, bf16[4,1024,256]{2,1,0:T(8,128)(2,1)} %constant.9.clone.table_low, ...), custom_call_target="tpu_custom_call" | custom-call | flops 1610612736 | bytes 10485760 | tf_op jit(solution)/shard_map/pallas_call | solution.py:572
  32.9 0.8 %copy.9 = f32[16,8,1024]{2,1,0:T(8,128)} copy(f32[16,8,1024]{2,1,0:T(8,128)S(1)} %shard_map.73) | data formatting | bytes 1048576
Async XLA Ops:
  0.0 0.7 %copy-start = (s32[32]{0:T(128)S(1)}, s32[32]{0:T(128)}, u32[]{:S(2)}) copy-start(s32[32]{0:T(128)} %param.9) | copy-start | bytes 388

commit v6 on v5

--- a/solution.py
+++ b/solution.py
@@ -349,9 +349,9 @@
             send_a[chunk, 4 * side + 2 * pair + 1] = odd.reshape(pairs, y_rows, width)
         if step == 0:
             pl.semaphore_wait(barrier, count)
-        if chunk == 0:
-            for target in far_targets if step == 0 else near_targets:
-                send_forward(0, target).start()
+        targets = far_targets if step % 2 == 0 else near_targets
+        for target in targets[:1] if step == 2 else targets:
+            send_forward(chunk, target).start()
         if step % 2 == 1:
             recv_a[chunk, me] = send_a[chunk, me]
 
@@ -439,9 +439,9 @@
         parts = mix(flat(value), flat(value))
         target[0], target[1] = (part.reshape(plane) for part in parts)
 
-    for target in others:
-        send_forward(0, target).wait_send()
-        send_forward(1, target).start()
+    for first, second in zip(far_targets[:3], far_targets[1:]):
+        send_forward(0, first).wait_send()
+        send_forward(1, second).start()
 
     low_plane = low_lanes.reshape(plane)
     first_lanes = jnp.logical_xor(low_plane, jnp.full(plane, half, jnp.int32) == 1)
@@ -542,11 +542,12 @@
                 total = total * focus_v[:, :, columns]
             result[:, :, columns] = total
 
-    for chunk in range(2):
-        for target in others:
-            if chunk == 1:
-                send_forward(1, target).wait_send()
-            send_back(chunk, target).wait_send()
+    for place, target in enumerate(others):
+        if place > 2:
+            send_forward(0, target).wait_send()
+        send_forward(1, target).wait_send()
+        send_back(0, target).wait_send()
+        send_back(1, target).wait_send()
 
 
 def kernel_body(residual, focus_bins, layer_class):
@@ -611,7 +612,7 @@
             dma((3,)),
         ],
         compiler_params=pltpu.CompilerParams(
-            collective_id=0, has_side_effects=True, vmem_limit_bytes=53 * 2**20
+            collective_id=0, has_side_effects=True, vmem_limit_bytes=54716 * 2**10
         ),
         cost_estimate=pl.CostEstimate(
             flops=2 * 6 * layers * y_rows * x_cells * x_cells,

time: 33.8 us -> 33.8 us (level)
  no operation moved by 1% of the time
where the time goes in v6:
time: 33.8 us; the launch traced here: 33.7 us
  Pallas kernels  32.2 us (95%)
  local copies, waits for them, and re-layouts  1.45 us (4%)
    pallas_call x1, Pallas kernels, kernel_body(): pl.pallas_call(kernel, out_shape=jax.ShapeDtypeStruct(residual.shape, f32...  32.2 us
    unnamed x3, local copies, waits for them, and re-layouts  1.45 us

profile of v6, /device:TPU:0, one launch (start us, length us, event | category | flops | bytes accessed | tf_op | source)
XLA Modules:
  0.0 33.7 jit_solution(13341261674825353945)
XLA Ops:
  0.0 0.0 copy-start
  0.0 0.7 %copy-done = s32[32]{0:T(128)S(1)} copy-done((s32[32]{0:T(128)S(1)}, s32[32]{0:T(128)}, u32[]{:S(2)}) %copy-start) | copy-done | bytes 152
  0.7 32.2 %shard_map.73 = f32[16,8,1024]{2,1,0:T(8,128)S(1)} custom-call(f32[16,8,1024]{2,1,0:T(8,128)} %residual.1, s32[16,8,1024]{2,1,0:T(8,128)} %bins.1, s32[1,32]{1,0:T(1,128)S(1)} %bitcast.1, bf16[4,1088,256]{2,1,0:T(8,128)(2,1)} %constant.8.clone.table_high, bf16[4,1024,256]{2,1,0:T(8,128)(2,1)} %constant.9.clone.table_low, ...), custom_call_target="tpu_custom_call" | custom-call | flops 1610612736 | bytes 10485760 | tf_op jit(solution)/shard_map/pallas_call | solution.py:573
  32.9 0.8 %copy.9 = f32[16,8,1024]{2,1,0:T(8,128)} copy(f32[16,8,1024]{2,1,0:T(8,128)S(1)} %shard_map.73) | data formatting | bytes 1048576
Async XLA Ops:
  0.0 0.7 %copy-start = (s32[32]{0:T(128)S(1)}, s32[32]{0:T(128)}, u32[]{:S(2)}) copy-start(s32[32]{0:T(128)} %param.9) | copy-start | bytes 388

commit v7 on v6

--- a/solution.py
+++ b/solution.py
@@ -236,13 +236,6 @@
     near = me // 4
     far = 1 - near
 
-    barrier = pltpu.get_barrier_semaphore()
-    for step in range(1, count):
-        pl.semaphore_signal(
-            barrier, inc=1, device_id={"hor": lax.rem(me + step, count)}, device_id_type=MESH
-        )
-    pl.semaphore_signal(barrier, inc=1, device_id={"dep": 1 - half}, device_id_type=MESH)
-
     def table_copy(kind, block):
         source = (table_high, table_low, back_high, back_low)[kind]
         target = (high_v, low_v, back_high_v, back_low_v)[kind]
@@ -265,7 +258,17 @@
     blocks = [far, near, 2 + far, 2 + near]
     for load in loads:
         load.start()
-    for block in blocks:
+    for kind in range(2):
+        table_copy(kind, far).start()
+
+    barrier = pltpu.get_barrier_semaphore()
+    for step in range(1, count):
+        pl.semaphore_signal(
+            barrier, inc=1, device_id={"hor": lax.rem(me + step, count)}, device_id_type=MESH
+        )
+    pl.semaphore_signal(barrier, inc=1, device_id={"dep": 1 - half}, device_id_type=MESH)
+
+    for block in blocks[1:]:
         table_copy(0, block).start()
         table_copy(1, block).start()
     for load in late_loads:
@@ -500,7 +503,7 @@
             value = transform_y(flat(first), flat(second))
             send_b[chunk, :, row] = value[:, :width].reshape(count, y_rows, width)
             send_b[chunk, :, row + 1] = value[:, width:].reshape(count, y_rows, width)
-        for target in others:
+        for target in [4 * far + step for step in range(4)] + near_targets:
             send_back(chunk, target).start()
         recv_b[chunk, me] = send_b[chunk, me]
 

time: 33.8 us -> 31.4 us (0.929)
  Pallas kernels: 32.2 us -> 29.6 us
    pallas_call x1, Pallas kernels: 32.2 us -> 29.6 us  [kernel_body(): pl.pallas_call(kernel, out_shape=jax.ShapeDtypeStruct(residual.shape, f32...]
where the time goes in v7:
time: 31.4 us; the launch traced here: 31.1 us
  Pallas kernels  29.6 us (94%)
  local copies, waits for them, and re-layouts  1.45 us (5%)
    pallas_call x1, Pallas kernels, kernel_body(): pl.pallas_call(kernel, out_shape=jax.ShapeDtypeStruct(residual.shape, f32...  29.6 us
    unnamed x3, local copies, waits for them, and re-layouts  1.45 us

profile of v7, /device:TPU:0, one launch (start us, length us, event | category | flops | bytes accessed | tf_op | source)
XLA Modules:
  0.0 31.1 jit_solution(5560388317311733079)
XLA Ops:
  0.0 0.0 copy-start
  0.0 0.7 %copy-done = s32[32]{0:T(128)S(1)} copy-done((s32[32]{0:T(128)S(1)}, s32[32]{0:T(128)}, u32[]{:S(2)}) %copy-start) | copy-done | bytes 152
  0.7 29.6 %shard_map.73 = f32[16,8,1024]{2,1,0:T(8,128)S(1)} custom-call(f32[16,8,1024]{2,1,0:T(8,128)} %residual.1, s32[16,8,1024]{2,1,0:T(8,128)} %bins.1, s32[1,32]{1,0:T(1,128)S(1)} %bitcast.1, bf16[4,1088,256]{2,1,0:T(8,128)(2,1)} %constant.8.clone.table_high, bf16[4,1024,256]{2,1,0:T(8,128)(2,1)} %constant.9.clone.table_low, ...), custom_call_target="tpu_custom_call" | custom-call | flops 1610612736 | bytes 10485760 | tf_op jit(solution)/shard_map/pallas_call | solution.py:576
  30.3 0.8 %copy.9 = f32[16,8,1024]{2,1,0:T(8,128)} copy(f32[16,8,1024]{2,1,0:T(8,128)S(1)} %shard_map.73) | data formatting | bytes 1048576
Async XLA Ops:
  0.0 0.7 %copy-start = (s32[32]{0:T(128)S(1)}, s32[32]{0:T(128)}, u32[]{:S(2)}) copy-start(s32[32]{0:T(128)} %param.9) | copy-start | bytes 388
